TPU v7x, 128 devices: a whole 4x4x4 slice. The times are simulated.
128 devices in a mesh: ctx: 4 (over x), head: 32 (over y, z, core).
Axes of the slice: x: 4, y: 4, z: 4, core: 2. Of those that a mesh axis runs over, the one named last changes fastest.
Arguments:
- hidden_rows: float32 [2048, 2304], P(('ctx', 'head')), may hold values from -60 to 60
- segment_ids: int32 [2048], replicated, may hold values from 0 to 1, never falling along the last dimension, each value on 1 to 1920 neighbouring positions
- w_query: float32 [2304, 6144], P(None, 'head'), may hold values from -0.125 to 0.125
- w_down: float32 [2304, 576], replicated, may hold values from -0.125 to 0.125
- w_up: float32 [512, 8192], P(None, 'head'), may hold values from -0.25 to 0.25
- w_out: float32 [4096, 2304], P('head'), may hold values from -0.09375 to 0.09375
Outputs:
- attended: float32 [2048, 2304], P(('ctx', 'head'))
- log_norm: float32 [32, 2048], P('head', 'ctx')
All inputs are finite; a program needn't handle non-finite values.
Results may differ from a plain program's by a relative error of at most 0.00015.
Values sent between devices are 32-bit elements; how exact they have to be, the bound alone decides.
A program may use at most 64 MiB of HBM per device.

v0:
```python
import math

import jax
import jax.numpy as jnp
from jax import lax
from jax.sharding import PartitionSpec as P

KV_RANK = 512
NOPE = 128
ROPE = 64
VDIM = 128


eps_norm = 1e-06
neg_fill = -1e30
precise = lax.Precision.HIGHEST


def joined_along(blocks, dim):
    blocks = jnp.moveaxis(blocks, 0, dim)
    lengths = blocks.shape
    return blocks.reshape(*lengths[:dim], lengths[dim] * lengths[dim + 1], *lengths[dim + 2 :])


def from_everyone(value, axis):
    copies = jnp.broadcast_to(value, (lax.axis_size(axis), *value.shape))
    return lax.all_to_all(copies, axis, split_axis=0, concat_axis=0, tiled=True)


def collect(value, axis, dim):
    return joined_along(from_everyone(value, axis), dim)


def from_behind(value, axis, steps):
    count = lax.axis_size(axis)
    first, last = (max(0, -steps), min(count, count - steps))
    return lax.ppermute(value, axis, [(source, source + steps) for source in range(first, last)])


def product(left, right):
    return jnp.dot(left, right, precision=precise, preferred_element_type=jnp.float32)


def normalize(raw_latent):
    compressed = raw_latent[:, :KV_RANK]
    mean_square = jnp.mean(compressed * compressed, axis=1, keepdims=True)
    return jnp.concatenate(
        [compressed * lax.rsqrt(mean_square + eps_norm), raw_latent[:, KV_RANK:]], axis=1
    )


def body(hidden_rows, segment_ids, w_query, w_down, w_up, w_out):
    ctx_count = lax.axis_size("ctx")
    ctx_at = lax.axis_index("ctx")
    head_count = w_query.shape[1] // (NOPE + ROPE)
    queries = product(lax.all_gather(hidden_rows, "head", axis=0, tiled=True), w_query)
    latent = collect(normalize(product(hidden_rows, w_down)), "head", 0)
    row_count = queries.shape[0]
    queries = queries.reshape(row_count, head_count, NOPE + ROPE).transpose(1, 0, 2)
    score_factor = 1.0 / math.sqrt(NOPE + ROPE)
    offsets = jnp.arange(row_count, dtype=jnp.int32)

    def attend(carry_state, query_heads, query_ctx, block, key_ctx):
        key_start = jnp.maximum(key_ctx, 0)
        query_pos = query_ctx * row_count + offsets
        key_pos = key_start * row_count + offsets
        query_seg = lax.dynamic_slice_in_dim(segment_ids, query_ctx * row_count, row_count)
        key_seg = lax.dynamic_slice_in_dim(segment_ids, key_start * row_count, row_count)
        allowed = (
            (key_pos[None, :] <= query_pos[:, None])
            & (key_seg[None, :] == query_seg[:, None])
            & (key_ctx >= 0)
        )
        up_proj = product(block[:, :KV_RANK], w_up).reshape(row_count, head_count, NOPE + VDIM)
        scores = jnp.einsum(
            "hqd,khd->hqk", query_heads[..., :NOPE], up_proj[..., :NOPE], precision=precise
        )
        scores = scores + jnp.einsum(
            "hqd,kd->hqk", query_heads[..., NOPE:], block[:, KV_RANK:], precision=precise
        )
        scores = jnp.where(allowed[None], scores * score_factor, neg_fill)
        peak_old, total_old, accum_old = carry_state
        peak_new = jnp.maximum(peak_old, jnp.max(scores, axis=2))
        weights = jnp.where(allowed[None], jnp.exp(scores - peak_new[..., None]), 0.0)
        factor = jnp.exp(peak_old - peak_new)
        total_new = total_old * factor + jnp.sum(weights, axis=2)
        accum_new = accum_old * factor[..., None] + jnp.einsum(
            "hqk,khd->hqd", weights, up_proj[..., NOPE:], precision=precise
        )
        return (peak_new, total_new, accum_new)

    start_state = (
        jnp.full((head_count, row_count), neg_fill, jnp.float32),
        jnp.zeros((head_count, row_count), jnp.float32),
        jnp.zeros((head_count, row_count, VDIM), jnp.float32),
    )
    carry_state = attend(start_state, queries, ctx_at, latent, ctx_at)
    moving = latent
    for hop_index in range(1, ctx_count):
        moving = from_behind(moving, "ctx", 1)
        key_ctx = ctx_at - hop_index
        carry_state = attend(carry_state, queries, ctx_at, moving, key_ctx)
    peak_final, total_final, accum_final = carry_state
    head_outputs = accum_final / total_final[..., None]
    log_norm = peak_final + jnp.log(total_final)
    flattened = head_outputs.transpose(1, 0, 2).reshape(row_count, head_count * VDIM)
    attended = lax.psum_scatter(product(flattened, w_out), "head", scatter_dimension=0, tiled=True)
    return (attended, log_norm)


def solution(mesh):
    in_specs = (
        P(("ctx", "head"), None),
        P(),
        P(None, "head"),
        P(),
        P(None, "head"),
        P("head", None),
    )
    out_specs = (P(("ctx", "head"), None), P("head", "ctx"))
    return jax.shard_map(body, mesh=mesh, in_specs=in_specs, out_specs=out_specs, check_vma=False)
```

profile of v0, /device:TPU:0, one launch (start us, length us, event | category | flops | bytes accessed | tf_op | source)
XLA Modules:
  0.0 263.5 jit_solution(4643689339331510467)
XLA Ops:
  8.0 7.0 %fusion.48 = f32[16,576]{1,0:T(8,128)S(1)} fusion(f32[16,2304]{1,0:T(8,128)} %param.6, f32[2304,576]{0,1:T(8,128)} %param.9), kind=kOutput, calls=%fused_computation.94 | convolution fusion | flops 254803968 | bytes 5492736 | tf_op jit(solution)/shard_map/dot_general | solution.py:41
  15.2 30.0 %all_to_all.5 = f32[32,16,576]{2,1,0:T(8,128)S(1)} all-to-all(f32[32,16,576]{2,1,0:T(8,128)S(1)} %broadcast_in_dim.24), channel_id=1, replica_groups=mesh['ctx'=4,'head'=32] {'head'}, dimensions={0} | all-to-all | bytes 2359296 | tf_op jit(solution)/shard_map/all_to_all | solution.py:27
  45.2 1.4 copy.9
  46.7 3.4 %collective-permute-start = (f32[512,576]{0,1:T(8,128)}, f32[512,576]{0,1:T(8,128)S(1)}, u32[]{:S(2)}, u32[]{:S(2)}) collective-permute-start(f32[512,576]{0,1:T(8,128)} %copy.9), channel_id=1, source_target_pairs={{0,32},{32,64},{64,96},{1,33},{33,65},{65,97},{2,34},{34,66},{66,9... | collective-permute-start | bytes 3538952 | tf_op jit(solution)/shard_map/ppermute | solution.py:37
  50.1 25.9 %collective-permute-done = f32[512,576]{0,1:T(8,128)S(1)} collective-permute-done((f32[512,576]{0,1:T(8,128)}, f32[512,576]{0,1:T(8,128)S(1)}, u32[]{:S(2)}, u32[]{:S(2)}) %collective-permute-start) | collective-permute-done | bytes 1179680 | tf_op jit(solution)/shard_map/ppermute | solution.py:37
  77.1 5.3 %collective-permute-start.1 = (f32[512,576]{0,1:T(8,128)S(1)}, f32[512,576]{0,1:T(8,128)}, u32[]{:S(2)}, u32[]{:S(2)}) collective-permute-start(f32[512,576]{0,1:T(8,128)S(1)} %collective-permute-done), channel_id=1, source_target_pairs={{0,32},{32,64},{64,96},{1,33},{33,65},{65,97},{2,34},{34,66},{66,9... | collective-permute-start | bytes 3538952 | tf_op jit(solution)/shard_map/ppermute | solution.py:37
  82.4 23.8 %collective-permute-done.1 = f32[512,576]{0,1:T(8,128)} collective-permute-done((f32[512,576]{0,1:T(8,128)S(1)}, f32[512,576]{0,1:T(8,128)}, u32[]{:S(2)}, u32[]{:S(2)}) %collective-permute-start.1) | collective-permute-done | bytes 1179680 | tf_op jit(solution)/shard_map/ppermute | solution.py:37
  106.2 5.5 %collective-permute-start.2 = (f32[512,576]{0,1:T(8,128)}, f32[512,576]{0,1:T(8,128)}, u32[]{:S(2)}, u32[]{:S(2)}) collective-permute-start(f32[512,576]{0,1:T(8,128)} %collective-permute-done.1), channel_id=1, source_target_pairs={{0,32},{32,64},{64,96},{1,33},{33,65},{65,97},{2,34},{34,66},{66,9... | collective-permute-start | bytes 3538952 | tf_op jit(solution)/shard_map/ppermute | solution.py:37
  111.9 3.0 %convolution_bitcast_fusion.3 = f32[512,1,256]{2,0,1:T(8,128)} fusion(f32[512,256]{1,0:T(8,128)} %param.10, f32[512,576]{1,0:T(8,128)S(1)} %bitcast.74), kind=kOutput, calls=%fused_computation.15 | convolution fusion | flops 805306368 | bytes 2097152 | tf_op jit(solution)/shard_map/dot_general | solution.py:41
  114.9 2.6 convolution_bitcast_fusion.2
  117.5 3.8 %convolution_bitcast_fusion.1 = f32[512,1,256]{2,0,1:T(8,128)} fusion(f32[512,256]{1,0:T(8,128)S(1)} %copy-done.1, f32[512,576]{0,1:T(8,128)} %collective-permute-done.1), kind=kOutput, calls=%fused_computation.13 | convolution fusion | flops 805306368 | bytes 2097152 | tf_op jit(solution)/shard_map/dot_general | solution.py:41
  121.3 13.7 %collective-permute-done.2 = f32[512,576]{0,1:T(8,128)} collective-permute-done((f32[512,576]{0,1:T(8,128)}, f32[512,576]{0,1:T(8,128)}, u32[]{:S(2)}, u32[]{:S(2)}) %collective-permute-start.2) | collective-permute-done | bytes 1179680 | tf_op jit(solution)/shard_map/ppermute | solution.py:37
  135.0 3.9 %convolution_bitcast_fusion = f32[512,1,256]{2,0,1:T(8,128)} fusion(f32[512,256]{1,0:T(8,128)S(1)} %copy-done.1, f32[512,576]{0,1:T(8,128)} %collective-permute-done.2), kind=kOutput, calls=%fused_computation.12 | convolution fusion | flops 805306368 | bytes 2097152 | tf_op jit(solution)/shard_map/dot_general | solution.py:41
  138.9 7.0 %convolution_bitcast_fusion.4 = f32[1,512,192]{1,2,0:T(8,128)S(1)} fusion(f32[512,2304]{1,0:T(8,128)} %all-gather.2.cloned.1.call-done, f32[2304,192]{0,1:T(8,128)S(1)} %copy-done), kind=kOutput, calls=%fused_computation.16 | convolution fusion | flops 2717908992 | bytes 6881280 | tf_op jit(solution)/shard_map/dot_general | solution.py:41
  151.2 2.2 fusion.46
  153.4 2.2 fusion.45
  155.6 2.2 fusion.44
  158.2 1.6 fusion.16
  159.8 2.1 fusion.11
  161.9 2.1 fusion.10
  164.1 2.1 fusion.9
  166.2 2.1 fusion.8
  168.3 5.4 %fusion.49 = f32[512,2304]{1,0:T(8,128)} fusion(f32[512,128]{1,0:T(8,128)S(1)} %fusion.8, f32[128,2304]{1,0:T(8,128)S(1)} %copy-done.4), kind=kOutput, calls=%fused_computation.95 | convolution fusion | flops 1811939328 | bytes 6160384 | tf_op jit(solution)/shard_map/dot_general | solution.py:41
  174.4 82.2 %reduce-scatter.2.cloned.1.call-done = f32[16,2304]{1,0:T(8,128)} async-done(((f32[512,2304]{1,0:T(8,128)}), f32[16,2304]{1,0:T(8,128)}) %reduce-scatter.2.cloned.1.call-update) | async-done | bytes 147472 | tf_op jit(solution)/shard_map/reduce_scatter | solution.py:107
  (44 shorter events, 8.5 us)
Async XLA Ops:
  7.2 131.7 %copy-start = (f32[2304,192]{0,1:T(8,128)S(1)}, f32[2304,192]{0,1:T(8,128)}, u32[]{:S(2)}) copy-start(f32[2304,192]{0,1:T(8,128)} %param.8) | copy-start | bytes 5308420
  7.2 131.7 %all-gather.2.cloned.1.call-start = ((), (), s32[]{:S(2)}) async-start(), calls=%async_computation.2 | async-start | bytes 4866048 | tf_op jit(solution)/shard_map/all_gather | solution.py:56
  7.9 248.7 %reduce-scatter.2.cloned.1.call-start = ((), (), s32[]{:S(2)}) async-start(), calls=%async_computation.3 | async-start | bytes 4866048 | tf_op jit(solution)/shard_map/reduce_scatter | solution.py:107
  45.2 66.5 %copy-start.9 = (s32[2048]{0:T(1024)S(1)}, s32[2048]{0:T(1024)}, u32[]{:S(2)}) copy-start(s32[2048]{0:T(1024)} %param.7) | copy-start | bytes 24580
  46.7 29.4 %collective-permute-start = (f32[512,576]{0,1:T(8,128)}, f32[512,576]{0,1:T(8,128)S(1)}, u32[]{:S(2)}, u32[]{:S(2)}) collective-permute-start(f32[512,576]{0,1:T(8,128)} %copy.9), channel_id=1, source_target_pairs={{0,32},{32,64},{64,96},{1,33},{33,65},{65,97},{2,34},{34,66},{66,9... | collective-permute-start | bytes 3538952 | tf_op jit(solution)/shard_map/ppermute | solution.py:37
  76.1 1.0 copy-start.2
  77.1 29.2 %collective-permute-start.1 = (f32[512,576]{0,1:T(8,128)S(1)}, f32[512,576]{0,1:T(8,128)}, u32[]{:S(2)}, u32[]{:S(2)}) collective-permute-start(f32[512,576]{0,1:T(8,128)S(1)} %collective-permute-done), channel_id=1, source_target_pairs={{0,32},{32,64},{64,96},{1,33},{33,65},{65,97},{2,34},{34,66},{66,9... | collective-permute-start | bytes 3538952 | tf_op jit(solution)/shard_map/ppermute | solution.py:37
  106.2 28.8 %collective-permute-start.2 = (f32[512,576]{0,1:T(8,128)}, f32[512,576]{0,1:T(8,128)}, u32[]{:S(2)}, u32[]{:S(2)}) collective-permute-start(f32[512,576]{0,1:T(8,128)} %collective-permute-done.1), channel_id=1, source_target_pairs={{0,32},{32,64},{64,96},{1,33},{33,65},{65,97},{2,34},{34,66},{66,9... | collective-permute-start | bytes 3538952 | tf_op jit(solution)/shard_map/ppermute | solution.py:37
  111.7 3.1 %copy-start.1 = (f32[512,256]{1,0:T(8,128)S(1)}, f32[512,256]{1,0:T(8,128)}, u32[]{:S(2)}) copy-start(f32[512,256]{1,0:T(8,128)} %param.10) | copy-start | bytes 1572868
  111.7 3.1 %copy-start.3 = (f32[512,576]{0,1:T(8,128)S(1)}, f32[512,576]{0,1:T(8,128)}, u32[]{:S(2)}) copy-start(f32[512,576]{0,1:T(8,128)} %copy-done.2) | copy-start | bytes 3538948
  138.9 7.0 %copy-start.8 = (f32[512,1,256]{2,0,1:T(8,128)S(1)}, f32[512,1,256]{2,0,1:T(8,128)}, u32[]{:S(2)}) copy-start(f32[512,1,256]{2,0,1:T(8,128)} %convolution_bitcast_fusion.3) | copy-start | bytes 1572868
  145.9 1.0 copy-start.7
  145.9 2.0 copy-start.6
  146.9 2.0 copy-start.5
  166.2 2.1 copy-start.4
Sparse Core Ops, SparseCore 0:
  10.3 56.2 all-gather.1
  173.9 82.6 reduce-scatter.1
where the time goes:
time: 264 us; the launch traced here: 263 us
  waiting for transfers between devices  146 us (55%)
  matrix products  52.9 us (20%)
  blocking collectives  30 us (11%)
  starting transfers between devices  14.4 us (5%)
  between operations  14.2 us (5%)
  other arithmetic  2.86 us (1%)
  local copies, waits for them, and re-layouts  2.71 us (1%)
    reduce_scatter x1, waiting for transfers between devices, body(): lax.psum_scatter(product(flattened, w_out), 'head', scatter_dimension=0,...  82.2 us
    ppermute x3, waiting for transfers between devices, from_behind(): lax.ppermute(value, axis, [(source, source + steps) for source in range(f...  63.5 us
    dot_general x7, matrix products, product(): jnp.dot(left, right, precision=precise, preferred_element_type=jnp.float32)  32.7 us
    all_to_all x1, blocking collectives, from_everyone(): return lax.all_to_all(copies, axis, split_axis=0, concat_axis=0, tiled=True)  30 us
    ppermute x3, starting transfers between devices, from_behind(): lax.ppermute(value, axis, [(source, source + steps) for source in range(f...  14.3 us
    dot_general x4, matrix products, attend(): jnp.einsum('hqk,khd->hqd', weights, up_proj[..., NOPE:], precision=precise)  8.48 us
    dot_general x4, matrix products, attend(): jnp.einsum('hqd,kd->hqk', query_heads[..., NOPE:], block[:, KV_RANK:], pr...  7.78 us
  transfers between devices with their start and end apart: 5, of which 4 were waited for; matrix products, arithmetic and copies ran while one was open for 9% of the time, Pallas kernels for 0%

commit v1 on v0

v1 whole, which is shorter than its diff:
```python
import functools
import math

import jax
import jax.numpy as jnp
from jax import lax
from jax.experimental import pallas as pl
from jax.experimental.pallas import tpu as pltpu
from jax.sharding import PartitionSpec as P

D = 2304
KV_RANK = 512
NOPE = 128
ROPE = 64
VDIM = 128
QK = NOPE + ROPE
TOK_CTX = 512
LAT = 640
HALF = D // 2

eps_norm = 1e-06
neg_fill = -1e30
f32 = jnp.float32
bf16 = jnp.bfloat16
MESH = pl.DeviceIdType.MESH
N_SEM = 160


def split(value):
    high = value.astype(bf16)
    return high, (value - high.astype(f32)).astype(bf16)


def dot(left, right, dims=((1,), (0,))):
    return lax.dot_general(left, right, (dims, ((), ())), preferred_element_type=f32)


def dot3(left, right, dims=((1,), (0,))):
    (left_high, left_low), (right_high, right_low) = left, right
    small = dot(left_high, right_low, dims) + dot(left_low, right_high, dims)
    return dot(left_high, right_high, dims) + small


def kernel(
    x_in, seg_in, wq_in, wd_in, wu_in, wo_in,
    out, ln_out,
    xs, lat, wq, wd, wu, wo, kv, kv_far, qh, ql, accq,
    top, tot, acc, part, relay, sums, relay2, sums2, red, ln, ln_far,
    send_sem, recv_sem, load_sem,
):
    ctx = lax.axis_index("ctx")
    head = lax.axis_index("head")
    core = lax.rem(head, 2)
    z0 = lax.rem(lax.div(head, 2), 4)
    y0 = lax.div(head, 8)

    def at(y, z):
        return (ctx, (y * 4 + z) * 2 + core)

    def turn(i, by):
        return lax.rem(i + by + 4, 4)

    ym, yp, yo = turn(y0, -1), turn(y0, 1), turn(y0, 2)
    zm, zp, zo = turn(z0, -1), turn(z0, 1), turn(z0, 2)
    Y_UP, Y_DOWN = at(yp, z0), at(ym, z0)
    Z_UP, Z_DOWN = at(y0, zp), at(y0, zm)
    PARTNER = (ctx, head + 1 - 2 * core)
    X_PEERS = [(turn(ctx, by), head) for by in (1, 2, 3)]

    barrier = pltpu.get_barrier_semaphore()
    peers = [Y_UP, Y_DOWN, Z_UP, Z_DOWN, PARTNER] + X_PEERS
    for peer in peers:
        pl.semaphore_signal(barrier, inc=1, device_id=peer, device_id_type=MESH)

    loads = []

    def load(src, dst):
        copy = pltpu.make_async_copy(src, dst, load_sem.at[len(loads)])
        copy.start()
        loads.append(copy)
        return copy

    load_x = load(x_in, xs.at[y0, z0])
    WD_STEPS = 3
    wd_rows = D // WD_STEPS
    load_wd = [
        load(wd_in.at[pl.ds(i * wd_rows, wd_rows)], wd.at[pl.ds(i * wd_rows, wd_rows)])
        for i in range(WD_STEPS)
    ]
    load_rest = [
        load(wq_in, wq.at[core]), load(wu_in, wu.at[core]), load(wo_in, wo.at[core])
    ]
    pl.semaphore_wait(barrier, len(peers))

    copies = []

    def send(src, dst, device):
        k = len(copies)
        copy = pltpu.make_async_remote_copy(
            src_ref=src, dst_ref=dst, send_sem=send_sem.at[k], recv_sem=recv_sem.at[k],
            device_id=device, device_id_type=MESH,
        )
        copy.start()
        copies.append(copy)
        return copy

    def gather(view, own=None):
        def hand(y, z, p, h, device):
            return send(view(y, z, p, h), view(y, z, p, h), device)

        first = view(y0, z0, None, None) if own is None else own
        target = view(y0, z0, None, None)
        y1 = send(first, target, Y_UP)
        y2 = send(first, target, Y_DOWN)
        z1 = send(first, target, Z_UP)
        z2 = send(first, target, Z_DOWN)
        yield
        y1.wait_recv()
        f1 = hand(ym, z0, None, 0, Y_UP)
        a = [hand(ym, z0, 0, None, Z_UP), hand(ym, z0, 0, None, Z_DOWN)]
        z1.wait_recv()
        g1 = hand(y0, zm, None, 0, Z_UP)
        b = [hand(y0, zm, 1, None, Y_UP), hand(y0, zm, 1, None, Y_DOWN)]
        y2.wait_recv()
        f2 = hand(yp, z0, None, 1, Y_DOWN)
        a += [hand(yp, z0, 0, None, Z_UP), hand(yp, z0, 0, None, Z_DOWN)]
        z2.wait_recv()
        g2 = hand(y0, zp, None, 1, Z_DOWN)
        b += [hand(y0, zp, 1, None, Y_UP), hand(y0, zp, 1, None, Y_DOWN)]
        yield
        f1.wait_recv()
        f2.wait_recv()
        a += [hand(yo, z0, 0, None, Z_UP), hand(yo, z0, 0, None, Z_DOWN)]
        g1.wait_recv()
        g2.wait_recv()
        b += [hand(y0, zo, 1, None, Y_UP), hand(y0, zo, 1, None, Y_DOWN)]
        yield
        last = []
        for i, (y, z) in enumerate(((ym, zm), (yp, zp), (yo, zo))):
            a[2 * i].wait_recv()
            last.append(hand(y, zm, 0, 0, Z_UP))
            b[2 * i].wait_recv()
            last.append(hand(ym, z, 1, 0, Y_UP))
            a[2 * i + 1].wait_recv()
            last.append(hand(y, zp, 0, 1, Z_DOWN))
            b[2 * i + 1].wait_recv()
            last.append(hand(yp, z, 1, 1, Y_DOWN))
        yield
        for copy in last:
            copy.wait_recv()
        yield

    everything = slice(None)

    def x_view(y, z, p, h):
        cols = everything if p is None else pl.ds(p * HALF, HALF)
        return xs.at[y, z, :, :, cols] if h is None else xs.at[y, z, h, :, cols]

    def lat_view(y, z, p, h):
        return lat.at[y, z, everything if p is None else p, everything if h is None else h]

    gather_x = gather(x_view, x_in)
    next(gather_x)
    load_x.wait()
    weight_copies = [
        send(wq_in, wq.at[core], PARTNER),
        send(wu_in, wu.at[core], PARTNER),
        send(wo_in, wo.at[core], PARTNER),
    ]

    own_high, own_low = split(xs[y0, z0].reshape(16, D))
    own_both = jnp.concatenate([own_high, own_low], axis=0)
    raw2 = jnp.zeros((32, KV_RANK + ROPE), f32)
    raw1 = jnp.zeros((16, KV_RANK + ROPE), f32)
    for i in range(WD_STEPS):
        load_wd[i].wait()
        w_high, w_low = split(wd[pl.ds(i * wd_rows, wd_rows), :])
        cols = slice(i * wd_rows, (i + 1) * wd_rows)
        raw2 = raw2 + dot(own_both[:, cols], w_high)
        raw1 = raw1 + dot(own_high[:, cols], w_low)
        if i == 0:
            next(gather_x)
    raw = raw2[:16] + (raw2[16:] + raw1)
    squeezed = raw[:, :KV_RANK]
    mean_square = jnp.mean(squeezed * squeezed, axis=1, keepdims=True)
    c_hi, c_lo = lax.div(ctx, 2), lax.rem(ctx, 2)
    lat[y0, z0, c_hi, c_lo, :, pl.ds(0, KV_RANK)] = squeezed * lax.rsqrt(mean_square + eps_norm)
    lat[y0, z0, c_hi, c_lo, :, pl.ds(KV_RANK, 128)] = jnp.concatenate(
        [raw[:, KV_RANK:], jnp.zeros((16, 64), f32)], axis=1
    )
    own_lat = lat.at[y0, z0, c_hi, c_lo]
    across = [send(own_lat, own_lat, peer) for peer in X_PEERS]
    next(gather_x)
    for copy in across:
        copy.wait_recv()
    gather_lat = gather(lat_view)
    next(gather_lat)
    next(gather_x)
    next(gather_lat)
    next(gather_x)
    next(gather_lat)

    for copy in load_rest:
        copy.wait()
    for copy in weight_copies:
        copy.wait_recv()

    accq[...] = jnp.zeros_like(accq)

    def query_columns(k, carry):
        cols = pl.ds(pl.multiple_of(k * 256, 256), 256)
        rows = split(xs[:, :, :, :, cols].reshape(256, 256))
        for h in range(2):
            accq[h] += dot3(rows, split(wq[h, cols, :]))
        return carry

    lax.fori_loop(0, 4, query_columns, 0)
    next(gather_lat)
    lax.fori_loop(4, D // 256, query_columns, 0)

    for h in range(2):
        qh[h], ql[h] = split(accq[h] * (1.0 / math.sqrt(QK)))

    ones = jnp.sum(seg_in[...], axis=(0, 1), keepdims=True)
    bound = 2048 - ones
    lane = lax.broadcasted_iota(jnp.int32, (1, 256), 1)
    q_pos = ctx * TOK_CTX + lax.div(lane, 16) * 32 + core * 16 + lax.rem(lane, 16)
    q_start = jnp.where(q_pos >= bound, bound, 0)
    row = lax.broadcasted_iota(jnp.int32, (128, 1), 0)
    row_block, row_ctx, row_in = lax.div(row, 32), lax.rem(lax.div(row, 16), 2), lax.rem(row, 16)

    top[...] = jnp.full_like(top, neg_fill)
    tot[...] = jnp.zeros_like(tot)
    acc[...] = jnp.zeros_like(acc)

    def attend(block, y, z, side):
        pos_a = row_ctx * TOK_CTX + (row_block * 4 + z) * 32 + row_in + side * 16
        pos_b = (row_ctx + 2) * TOK_CTX + (y * 4 + row_block) * 32 + row_in + side * 16
        k_pos = jnp.concatenate([pos_a, pos_b], axis=0)
        allowed = (k_pos <= q_pos) & (k_pos >= q_start)
        for h in range(2):
            keys = jnp.concatenate(
                [block[:, h * 256 : h * 256 + NOPE], block[:, 512 : 512 + ROPE]], axis=1
            )
            scores = dot3(split(keys), (qh[h], ql[h]), ((1,), (1,)))
            scores = jnp.where(allowed, scores, neg_fill)
            old = top[h]
            new = jnp.maximum(old, jnp.max(scores, axis=0, keepdims=True))
            weights = jnp.where(allowed, jnp.exp(scores - new), 0.0)
            factor = jnp.exp(old - new)
            top[h] = new
            tot[h] = tot[h] * factor + jnp.sum(weights, axis=0, keepdims=True)
            values = block[:, h * 256 + NOPE : (h + 1) * 256].T
            acc[h] = acc[h] * factor + dot3(split(values), split(weights))

    def make(g, y, z):
        block_a = lat[:, z, 0].reshape(128, LAT)
        block_b = lat[y, :, 1].reshape(128, LAT)
        block = jnp.concatenate([block_a, block_b], axis=0)
        both = split(block[:, :KV_RANK])
        for h in range(2):
            kv[g, :, pl.ds(h * 256, 256)] = dot3(both, split(wu[h]))
        kv[g, :, pl.ds(512, 128)] = block[:, KV_RANK:]
        return send(kv.at[g], kv_far.at[g], PARTNER)

    first = make(0, y0, z0)
    attend(kv[0], y0, z0, core)
    first.wait_recv()
    attend(kv_far[0], y0, z0, 1 - core)
    steps = [make(1, ym, zm), make(2, yp, zp)]
    for g, (y, z) in ((1, (ym, zm)), (2, (yp, zp))):
        attend(kv[g], y, z, core)
        steps[g - 1].wait_recv()
        attend(kv_far[g], y, z, 1 - core)
    next(gather_lat)
    final = make(3, yo, zo)
    attend(kv[3], yo, zo, core)
    final.wait_recv()
    attend(kv_far[3], yo, zo, 1 - core)

    heads = []
    for h in range(2):
        ln[h] = jnp.broadcast_to(top[h] + jnp.log(tot[h]), (8, 256))
        heads.append(acc[h] / tot[h])
    ln_copy = send(ln.at[1 - core], ln_far, PARTNER)
    rows = split(jnp.concatenate(heads, axis=0).T)

    axes = (((zm, z0, zp, zo), Z_DOWN, Z_UP), ((ym, y0, yp, yo), Y_DOWN, Y_UP))

    def blocks(p, u, v):
        cols = pl.ds(p * HALF, HALF)
        return part.at[v, u, :, :, cols] if p == 0 else part.at[u, v, :, :, cols]

    low, high = pl.ds(0, 2), pl.ds(2, 2)
    waits = []
    for p in range(2):
        (um, u0, up, uo), down, upward = axes[p]
        tile = HALF // 3
        for t in range(3):
            cols = pl.ds(p * HALF + t * tile, tile)
            w_out = split(wo[:, :, cols].reshape(256, tile))
            part[:, :, :, :, cols] = dot3(rows, w_out).reshape(4, 4, 2, 8, tile)
        waits.append([
            send(blocks(p, uo, low), relay.at[p, 0], upward),
            send(blocks(p, uo, high), relay.at[p, 1], down),
            send(blocks(p, up, high), sums.at[p, 0, high], upward),
            send(blocks(p, um, low), sums.at[p, 1, low], down),
        ])
    for p in range(2):
        (um, u0, up, uo), down, upward = axes[p]
        waits[p][0].wait_recv()
        blocks(p, up, low)[...] += relay[p, 0]
        waits[p].append(send(blocks(p, up, low), sums.at[p, 0, low], upward))
        waits[p][1].wait_recv()
        blocks(p, um, high)[...] += relay[p, 1]
        waits[p].append(send(blocks(p, um, high), sums.at[p, 1, high], down))
    waits2 = []
    for p in range(2):
        (um, u0, up, uo), down, upward = axes[1 - p]
        for copy in waits[p][2:]:
            copy.wait_recv()
        red[p] = blocks(p, axes[p][0][1], pl.ds(0, 4))[...] + (sums[p, 0] + sums[p, 1])
        waits2.append([
            send(red.at[p, uo, 0], relay2.at[p, 0], upward),
            send(red.at[p, uo, 1], relay2.at[p, 1], down),
            send(red.at[p, up, 1], sums2.at[p, 0, 1], upward),
            send(red.at[p, um, 0], sums2.at[p, 1, 0], down),
        ])
    for p in range(2):
        (um, u0, up, uo), down, upward = axes[1 - p]
        waits2[p][0].wait_recv()
        red[p, up, 0] += relay2[p, 0]
        waits2[p].append(send(red.at[p, up, 0], sums2.at[p, 0, 0], upward))
        waits2[p][1].wait_recv()
        red[p, um, 1] += relay2[p, 1]
        waits2[p].append(send(red.at[p, um, 1], sums2.at[p, 1, 1], down))
    ln_copy.wait_recv()
    ln_out[core] = ln[core]
    ln_out[1 - core] = ln_far[...]
    for p in range(2):
        for copy in waits2[p][2:]:
            copy.wait_recv()
        out[:, :, pl.ds(p * HALF, HALF)] = red[p, axes[1 - p][0][1]] + (sums2[p, 0] + sums2[p, 1])
    for copy in copies:
        copy.wait_send()


def body(hidden_rows, segment_ids, w_query, w_down, w_up, w_out):
    any_space = pl.BlockSpec(memory_space=pl.ANY)
    vmem = pl.BlockSpec(memory_space=pltpu.VMEM)
    out, ln = pl.pallas_call(
        kernel,
        out_shape=(
            jax.ShapeDtypeStruct((2, 8, D), f32),
            jax.ShapeDtypeStruct((2, 8, 256), f32),
        ),
        in_specs=[any_space, vmem, any_space, any_space, any_space, any_space],
        out_specs=(vmem, vmem),
        scratch_shapes=[
            pltpu.VMEM((4, 4, 2, 8, D), f32),
            pltpu.VMEM((4, 4, 2, 2, 16, LAT), f32),
            pltpu.VMEM((2, D, QK), f32),
            pltpu.VMEM((D, KV_RANK + ROPE), f32),
            pltpu.VMEM((2, KV_RANK, 256), f32),
            pltpu.VMEM((2, VDIM, D), f32),
            pltpu.VMEM((4, 256, LAT), f32),
            pltpu.VMEM((4, 256, LAT), f32),
            pltpu.VMEM((2, 256, QK), bf16),
            pltpu.VMEM((2, 256, QK), bf16),
            pltpu.VMEM((2, 256, QK), f32),
            pltpu.VMEM((2, 1, 256), f32),
            pltpu.VMEM((2, 1, 256), f32),
            pltpu.VMEM((2, VDIM, 256), f32),
            pltpu.VMEM((4, 4, 2, 8, D), f32),
            pltpu.VMEM((2, 2, 2, 2, 8, HALF), f32),
            pltpu.VMEM((2, 2, 4, 2, 8, HALF), f32),
            pltpu.VMEM((2, 2, 8, HALF), f32),
            pltpu.VMEM((2, 2, 2, 8, HALF), f32),
            pltpu.VMEM((2, 4, 2, 8, HALF), f32),
            pltpu.VMEM((2, 8, 256), f32),
            pltpu.VMEM((8, 256), f32),
            pltpu.SemaphoreType.DMA((N_SEM,)),
            pltpu.SemaphoreType.DMA((N_SEM,)),
            pltpu.SemaphoreType.DMA((8,)),
        ],
        compiler_params=pltpu.CompilerParams(
            collective_id=0, has_side_effects=True, vmem_limit_bytes=58 * 1024 * 1024
        ),
        name="latent_attention",
    )(
        hidden_rows.reshape(2, 8, D), segment_ids.reshape(16, 128),
        w_query, w_down, w_up, w_out,
    )
    log_norm = ln[:, 0, :].reshape(2, 16, 16).transpose(1, 0, 2).reshape(1, TOK_CTX)
    return out.reshape(16, D), log_norm


def solution(mesh):
    in_specs = (
        P(("ctx", "head"), None),
        P(),
        P(None, "head"),
        P(),
        P(None, "head"),
        P("head", None),
    )
    out_specs = (P(("ctx", "head"), None), P("head", "ctx"))
    return jax.shard_map(body, mesh=mesh, in_specs=in_specs, out_specs=out_specs, check_vma=False)
```

time: 264 us -> 90.1 us (0.34)
  waiting for transfers between devices: 146 us -> 0 us
  Pallas kernels: 0 us -> 76.7 us
  matrix products: 52.9 us -> 0 us
  blocking collectives: 30 us -> 0 us
  starting transfers between devices: 14.4 us -> 0 us
  between operations: 14.2 us -> 0.65 us
  local copies, waits for them, and re-layouts: 2.71 us -> 12.4 us
  other arithmetic: 2.86 us -> 0 us
    reduce_scatter x1 -> x0, waiting for transfers between devices: 82.2 us -> none  [body(): lax.psum_scatter(product(flattened, w_out), 'head', scatter_dimension=0,...]
    pallas_call x0 -> x1, Pallas kernels: none -> 76.7 us  [body(): pl.pallas_call(kernel, out_shape=(jax.ShapeDtypeStruct((2, 8, D), f32), j...]
    ppermute x3 -> x0, waiting for transfers between devices: 63.5 us -> none  [from_behind(): lax.ppermute(value, axis, [(source, source + steps) for source in range(f...]
    dot_general x19 -> x0, matrix products: 52.9 us -> none  [the longest x7 32.7 us: product(): jnp.dot(left, right, precision=precise, preferred_element_type=jnp.float32)]
    all_to_all x1 -> x0, blocking collectives: 30 us -> none  [from_everyone(): return lax.all_to_all(copies, axis, split_axis=0, concat_axis=0, tiled=True)]
    ppermute x3 -> x0, starting transfers between devices: 14.3 us -> none  [from_behind(): lax.ppermute(value, axis, [(source, source + steps) for source in range(f...]
    unnamed x20 -> x3, local copies, waits for them, and re-layouts: 1.07 us -> 10.9 us
  transfers between devices with their start and end apart: 5 -> 0, of which waited for: 4 -> 0; matrix products, arithmetic and copies ran while one was open for 9% -> 0% of each run, Pallas kernels for 0% -> 0%
where the time goes in v1:
time: 90.1 us; the launch traced here: 89.7 us
  Pallas kernels  76.7 us (85%)
  local copies, waits for them, and re-layouts  12.4 us (14%)
    pallas_call x1, Pallas kernels, body(): pl.pallas_call(kernel, out_shape=(jax.ShapeDtypeStruct((2, 8, D), f32), j...  76.7 us
    unnamed x3, local copies, waits for them, and re-layouts  10.9 us

profile of v1, /device:TPU:0, one launch (start us, length us, event | category | flops | bytes accessed | tf_op | source)
XLA Modules:
  0.0 89.7 jit_solution(12363226563870687770)
XLA Ops:
  0.6 3.0 %copy.8.wq_in = f32[2304,192]{1,0:T(8,128)} copy(f32[2304,192]{0,1:T(8,128)} %param.8) | data formatting | bytes 3538944 | tf_op args[2]
  3.6 6.4 %copy.9.wd_in = f32[2304,576]{1,0:T(8,128)} copy(f32[2304,576]{0,1:T(8,128)} %param.9) | data formatting | bytes 10616832 | tf_op args[3]
  10.0 76.7 %latent_attention.1 = (f32[2,8,2304]{2,1,0:T(8,128)}, f32[2,8,256]{2,1,0:T(8,128)}) custom-call(f32[2,8,2304]{2,1,0:T(8,128)} %bitcast.5, s32[16,128]{1,0:T(8,128)} %bitcast.7, f32[2304,192]{1,0:T(8,128)} %copy.8.wq_in, f32[2304,576]{1,0:T(8,128)} %copy.9.wd_in, f32[512,256]{1,0:T(8,128)} %wu_in.1, f32[128,2304]{1,0:T(8,128)} %wo_in.1), custom_call_target="tpu_custom_call" | custom-call | tf_op jit(solution)/shard_map/latent_attention/pallas_call | solution.py:351
  86.7 0.7 slice_reduce_fusion
  87.4 0.1 reshape_squeeze.3
  87.5 0.7 reshape.19
  88.2 1.6 %copy.12 = f32[16,2304]{1,0:T(8,128)} copy(f32[16,2304]{1,0:T(8,128)} %bitcast.4) | data formatting | bytes 294912
  (1 shorter events, 0.0 us)

commit v2 on v1

--- a/solution.py
+++ b/solution.py
@@ -45,7 +45,7 @@
     x_in, seg_in, wq_in, wd_in, wu_in, wo_in,
     out, ln_out,
     xs, lat, wq, wd, wu, wo, kv, kv_far, qh, ql, accq,
-    top, tot, acc, part, relay, sums, relay2, sums2, red, ln, ln_far,
+    top, tot, acc, part, relay, sums, sums2, red, ln, ln_far,
     send_sem, recv_sem, load_sem,
 ):
     ctx = lax.axis_index("ctx")
@@ -64,11 +64,12 @@
     zm, zp, zo = turn(z0, -1), turn(z0, 1), turn(z0, 2)
     Y_UP, Y_DOWN = at(yp, z0), at(ym, z0)
     Z_UP, Z_DOWN = at(y0, zp), at(y0, zm)
+    Y_OPP, Z_OPP = at(yo, z0), at(y0, zo)
     PARTNER = (ctx, head + 1 - 2 * core)
     X_PEERS = [(turn(ctx, by), head) for by in (1, 2, 3)]
 
     barrier = pltpu.get_barrier_semaphore()
-    peers = [Y_UP, Y_DOWN, Z_UP, Z_DOWN, PARTNER] + X_PEERS
+    peers = [Y_UP, Y_DOWN, Z_UP, Z_DOWN, Y_OPP, Z_OPP, PARTNER] + X_PEERS
     for peer in peers:
         pl.semaphore_signal(barrier, inc=1, device_id=peer, device_id_type=MESH)
 
@@ -84,7 +85,7 @@
     WD_STEPS = 3
     wd_rows = D // WD_STEPS
     load_wd = [
-        load(wd_in.at[pl.ds(i * wd_rows, wd_rows)], wd.at[pl.ds(i * wd_rows, wd_rows)])
+        load(wd_in.at[:, pl.ds(i * wd_rows, wd_rows)], wd.at[:, pl.ds(i * wd_rows, wd_rows)])
         for i in range(WD_STEPS)
     ]
     load_rest = [
@@ -109,30 +110,21 @@
             return send(view(y, z, p, h), view(y, z, p, h), device)
 
         first = view(y0, z0, None, None) if own is None else own
-        target = view(y0, z0, None, None)
-        y1 = send(first, target, Y_UP)
-        y2 = send(first, target, Y_DOWN)
-        z1 = send(first, target, Z_UP)
-        z2 = send(first, target, Z_DOWN)
+        near = [
+            send(first, view(y0, z0, None, None), device)
+            for device in (Y_UP, Z_UP, Y_DOWN, Z_DOWN, Y_OPP, Z_OPP)
+        ]
         yield
-        y1.wait_recv()
-        f1 = hand(ym, z0, None, 0, Y_UP)
-        a = [hand(ym, z0, 0, None, Z_UP), hand(ym, z0, 0, None, Z_DOWN)]
-        z1.wait_recv()
-        g1 = hand(y0, zm, None, 0, Z_UP)
-        b = [hand(y0, zm, 1, None, Y_UP), hand(y0, zm, 1, None, Y_DOWN)]
-        y2.wait_recv()
-        f2 = hand(yp, z0, None, 1, Y_DOWN)
-        a += [hand(yp, z0, 0, None, Z_UP), hand(yp, z0, 0, None, Z_DOWN)]
-        z2.wait_recv()
-        g2 = hand(y0, zp, None, 1, Z_DOWN)
-        b += [hand(y0, zp, 1, None, Y_UP), hand(y0, zp, 1, None, Y_DOWN)]
+        a, b = [], []
+        for k, i, j in ((0, ym, zm), (2, yp, zp)):
+            near[k].wait_recv()
+            a += [hand(i, z0, 0, None, Z_UP), hand(i, z0, 0, None, Z_DOWN)]
+            near[k + 1].wait_recv()
+            b += [hand(y0, j, 1, None, Y_UP), hand(y0, j, 1, None, Y_DOWN)]
         yield
-        f1.wait_recv()
-        f2.wait_recv()
+        near[4].wait_recv()
         a += [hand(yo, z0, 0, None, Z_UP), hand(yo, z0, 0, None, Z_DOWN)]
-        g1.wait_recv()
-        g2.wait_recv()
+        near[5].wait_recv()
         b += [hand(y0, zo, 1, None, Y_UP), hand(y0, zo, 1, None, Y_DOWN)]
         yield
         last = []
@@ -174,20 +166,21 @@
     raw1 = jnp.zeros((16, KV_RANK + ROPE), f32)
     for i in range(WD_STEPS):
         load_wd[i].wait()
-        w_high, w_low = split(wd[pl.ds(i * wd_rows, wd_rows), :])
+        w_high, w_low = split(wd[:, pl.ds(i * wd_rows, wd_rows)])
         cols = slice(i * wd_rows, (i + 1) * wd_rows)
-        raw2 = raw2 + dot(own_both[:, cols], w_high)
-        raw1 = raw1 + dot(own_high[:, cols], w_low)
+        raw2 = raw2 + dot(own_both[:, cols], w_high, ((1,), (1,)))
+        raw1 = raw1 + dot(own_high[:, cols], w_low, ((1,), (1,)))
         if i == 0:
             next(gather_x)
     raw = raw2[:16] + (raw2[16:] + raw1)
     squeezed = raw[:, :KV_RANK]
     mean_square = jnp.mean(squeezed * squeezed, axis=1, keepdims=True)
     c_hi, c_lo = lax.div(ctx, 2), lax.rem(ctx, 2)
-    lat[y0, z0, c_hi, c_lo, :, pl.ds(0, KV_RANK)] = squeezed * lax.rsqrt(mean_square + eps_norm)
-    lat[y0, z0, c_hi, c_lo, :, pl.ds(KV_RANK, 128)] = jnp.concatenate(
-        [raw[:, KV_RANK:], jnp.zeros((16, 64), f32)], axis=1
-    )
+    squeezed = squeezed * lax.rsqrt(mean_square + eps_norm)
+    for j in range(4):
+        tiles = squeezed[:, j * 128 : (j + 1) * 128].reshape(2, 8, 128)
+        lat[y0, z0, c_hi, c_lo, pl.ds(2 * j, 2)] = tiles
+    lat[y0, z0, c_hi, c_lo, 8] = jnp.concatenate([raw[:8, KV_RANK:], raw[8:, KV_RANK:]], axis=1)
     own_lat = lat.at[y0, z0, c_hi, c_lo]
     across = [send(own_lat, own_lat, peer) for peer in X_PEERS]
     next(gather_x)
@@ -211,7 +204,7 @@
         cols = pl.ds(pl.multiple_of(k * 256, 256), 256)
         rows = split(xs[:, :, :, :, cols].reshape(256, 256))
         for h in range(2):
-            accq[h] += dot3(rows, split(wq[h, cols, :]))
+            accq[h] += dot3(rows, split(wq[h, :, cols]), ((1,), (1,)))
         return carry
 
     lax.fori_loop(0, 4, query_columns, 0)
@@ -254,13 +247,17 @@
             acc[h] = acc[h] * factor + dot3(split(values), split(weights))
 
     def make(g, y, z):
-        block_a = lat[:, z, 0].reshape(128, LAT)
-        block_b = lat[y, :, 1].reshape(128, LAT)
-        block = jnp.concatenate([block_a, block_b], axis=0)
-        both = split(block[:, :KV_RANK])
+        def columns(tiles):
+            pair = [lat[:, z, 0, :, tiles], lat[y, :, 1, :, tiles]]
+            return jnp.concatenate([value.reshape(-1, 128) for value in pair], axis=0)
+
+        both = split(jnp.concatenate([columns(pl.ds(2 * j, 2)) for j in range(4)], axis=1))
         for h in range(2):
             kv[g, :, pl.ds(h * 256, 256)] = dot3(both, split(wu[h]))
-        kv[g, :, pl.ds(512, 128)] = block[:, KV_RANK:]
+        shared = columns(8).reshape(16, 8, 128)
+        shared = jnp.concatenate([shared[:, :, :64], shared[:, :, 64:]], axis=1).reshape(256, 64)
+        kv[g, :, pl.ds(512, 64)] = shared
+        kv[g, :, pl.ds(576, 64)] = jnp.zeros((256, 64), f32)
         return send(kv.at[g], kv_far.at[g], PARTNER)
 
     first = make(0, y0, z0)
@@ -285,62 +282,84 @@
     ln_copy = send(ln.at[1 - core], ln_far, PARTNER)
     rows = split(jnp.concatenate(heads, axis=0).T)
 
-    axes = (((zm, z0, zp, zo), Z_DOWN, Z_UP), ((ym, y0, yp, yo), Y_DOWN, Y_UP))
-
-    def blocks(p, u, v):
+    on_z = ((zm, z0, zp, zo), Z_DOWN, Z_UP, Z_OPP)
+    on_y = ((ym, y0, yp, yo), Y_DOWN, Y_UP, Y_OPP)
+    axes = (on_z, on_y)
+
+    def order(p):
+        vm, v0, vp, vo = axes[1 - p][0]
+        return vo, vm, vp, v0
+
+    def rows_of(p, u, i, h):
         cols = pl.ds(p * HALF, HALF)
-        return part.at[v, u, :, :, cols] if p == 0 else part.at[u, v, :, :, cols]
-
-    low, high = pl.ds(0, 2), pl.ds(2, 2)
-    waits = []
+        v = order(p)[i]
+        return part.at[v, u, h, :, cols] if p == 0 else part.at[u, v, h, :, cols]
+
+    relays, direct, second, final2 = {}, {}, {}, {}
     for p in range(2):
-        (um, u0, up, uo), down, upward = axes[p]
+        (um, u0, up, uo), down, upward, _ = axes[p]
         tile = HALF // 3
         for t in range(3):
             cols = pl.ds(p * HALF + t * tile, tile)
             w_out = split(wo[:, :, cols].reshape(256, tile))
             part[:, :, :, :, cols] = dot3(rows, w_out).reshape(4, 4, 2, 8, tile)
-        waits.append([
-            send(blocks(p, uo, low), relay.at[p, 0], upward),
-            send(blocks(p, uo, high), relay.at[p, 1], down),
-            send(blocks(p, up, high), sums.at[p, 0, high], upward),
-            send(blocks(p, um, low), sums.at[p, 1, low], down),
-        ])
+        for i in range(4):
+            relays[p, i] = (
+                send(rows_of(p, uo, i, 0), relay.at[p, 0, i], upward),
+                send(rows_of(p, uo, i, 1), relay.at[p, 1, i], down),
+            )
+        for i in range(4):
+            direct[p, i] = (
+                send(rows_of(p, up, i, 1), sums.at[p, 0, i, 1], upward),
+                send(rows_of(p, um, i, 0), sums.at[p, 1, i, 0], down),
+            )
+
+    def pass_on(p, i):
+        (um, u0, up, uo), down, upward, _ = axes[p]
+        relays[p, i][0].wait_recv()
+        rows_of(p, up, i, 0)[...] += relay[p, 0, i]
+        one = send(rows_of(p, up, i, 0), sums.at[p, 0, i, 0], upward)
+        relays[p, i][1].wait_recv()
+        rows_of(p, um, i, 1)[...] += relay[p, 1, i]
+        second[p, i] = (one, send(rows_of(p, um, i, 1), sums.at[p, 1, i, 1], down))
+
+    def finish(p, i):
+        u0 = axes[p][0][1]
+        _, down, upward, opposite = axes[1 - p]
+        for copy in (*direct[p, i], *second[p, i]):
+            copy.wait_recv()
+        for h in range(2):
+            red[p, i, h] = rows_of(p, u0, i, h)[...] + (sums[p, 0, i, h] + sums[p, 1, i, h])
+        if i < 3:
+            device = (opposite, down, upward)[i]
+            final2[p, i] = send(red.at[p, i], sums2.at[p, i], device)
+
+    for stage in range(6):
+        for p in range(2):
+            if stage < 4:
+                pass_on(p, stage)
+            if stage >= 2:
+                finish(p, stage - 2)
+
+    ln_copy.wait_recv()
+    from_lane = lax.broadcasted_iota(jnp.int32, (256, 512), 0)
+    to_lane = lax.broadcasted_iota(jnp.int32, (256, 512), 1)
+    to_own = lax.div(from_lane, 16) * 32 + lax.rem(from_lane, 16)
+    placed = jnp.zeros((8, 512), f32)
+    for value, side in ((ln[core], core), (ln_far[...], 1 - core)):
+        place = jnp.where(to_lane == to_own + side * 16, 1.0, 0.0).astype(bf16)
+        high, rest = value.astype(bf16), value
+        rest = rest - high.astype(f32)
+        middle = rest.astype(bf16)
+        lowest = (rest - middle.astype(f32)).astype(bf16)
+        placed = placed + ((dot(high, place) + dot(middle, place)) + dot(lowest, place))
+    ln_out[...] = placed[:1]
+
     for p in range(2):
-        (um, u0, up, uo), down, upward = axes[p]
-        waits[p][0].wait_recv()
-        blocks(p, up, low)[...] += relay[p, 0]
-        waits[p].append(send(blocks(p, up, low), sums.at[p, 0, low], upward))
-        waits[p][1].wait_recv()
-        blocks(p, um, high)[...] += relay[p, 1]
-        waits[p].append(send(blocks(p, um, high), sums.at[p, 1, high], down))
-    waits2 = []
-    for p in range(2):
-        (um, u0, up, uo), down, upward = axes[1 - p]
-        for copy in waits[p][2:]:
-            copy.wait_recv()
-        red[p] = blocks(p, axes[p][0][1], pl.ds(0, 4))[...] + (sums[p, 0] + sums[p, 1])
-        waits2.append([
-            send(red.at[p, uo, 0], relay2.at[p, 0], upward),
-            send(red.at[p, uo, 1], relay2.at[p, 1], down),
-            send(red.at[p, up, 1], sums2.at[p, 0, 1], upward),
-            send(red.at[p, um, 0], sums2.at[p, 1, 0], down),
-        ])
-    for p in range(2):
-        (um, u0, up, uo), down, upward = axes[1 - p]
-        waits2[p][0].wait_recv()
-        red[p, up, 0] += relay2[p, 0]
-        waits2[p].append(send(red.at[p, up, 0], sums2.at[p, 0, 0], upward))
-        waits2[p][1].wait_recv()
-        red[p, um, 1] += relay2[p, 1]
-        waits2[p].append(send(red.at[p, um, 1], sums2.at[p, 1, 1], down))
-    ln_copy.wait_recv()
-    ln_out[core] = ln[core]
-    ln_out[1 - core] = ln_far[...]
-    for p in range(2):
-        for copy in waits2[p][2:]:
-            copy.wait_recv()
-        out[:, :, pl.ds(p * HALF, HALF)] = red[p, axes[1 - p][0][1]] + (sums2[p, 0] + sums2[p, 1])
+        for i in range(3):
+            final2[p, i].wait_recv()
+        total = red[p, 3] + sums2[p, 0] + (sums2[p, 1] + sums2[p, 2])
+        out[:, :, pl.ds(p * HALF, HALF)] = total
     for copy in copies:
         copy.wait_send()
 
@@ -352,15 +371,15 @@
         kernel,
         out_shape=(
             jax.ShapeDtypeStruct((2, 8, D), f32),
-            jax.ShapeDtypeStruct((2, 8, 256), f32),
+            jax.ShapeDtypeStruct((1, TOK_CTX), f32),
         ),
         in_specs=[any_space, vmem, any_space, any_space, any_space, any_space],
         out_specs=(vmem, vmem),
         scratch_shapes=[
             pltpu.VMEM((4, 4, 2, 8, D), f32),
-            pltpu.VMEM((4, 4, 2, 2, 16, LAT), f32),
-            pltpu.VMEM((2, D, QK), f32),
-            pltpu.VMEM((D, KV_RANK + ROPE), f32),
+            pltpu.VMEM((4, 4, 2, 2, 9, 8, 128), f32),
+            pltpu.VMEM((2, QK, D), f32),
+            pltpu.VMEM((KV_RANK + ROPE, D), f32),
             pltpu.VMEM((2, KV_RANK, 256), f32),
             pltpu.VMEM((2, VDIM, D), f32),
             pltpu.VMEM((4, 256, LAT), f32),
@@ -372,10 +391,9 @@
             pltpu.VMEM((2, 1, 256), f32),
             pltpu.VMEM((2, VDIM, 256), f32),
             pltpu.VMEM((4, 4, 2, 8, D), f32),
-            pltpu.VMEM((2, 2, 2, 2, 8, HALF), f32),
+            pltpu.VMEM((2, 2, 4, 8, HALF), f32),
             pltpu.VMEM((2, 2, 4, 2, 8, HALF), f32),
-            pltpu.VMEM((2, 2, 8, HALF), f32),
-            pltpu.VMEM((2, 2, 2, 8, HALF), f32),
+            pltpu.VMEM((2, 3, 2, 8, HALF), f32),
             pltpu.VMEM((2, 4, 2, 8, HALF), f32),
             pltpu.VMEM((2, 8, 256), f32),
             pltpu.VMEM((8, 256), f32),
@@ -389,10 +407,9 @@
         name="latent_attention",
     )(
         hidden_rows.reshape(2, 8, D), segment_ids.reshape(16, 128),
-        w_query, w_down, w_up, w_out,
+        w_query.T, w_down.T, w_up, w_out,
     )
-    log_norm = ln[:, 0, :].reshape(2, 16, 16).transpose(1, 0, 2).reshape(1, TOK_CTX)
-    return out.reshape(16, D), log_norm
+    return out.reshape(16, D), ln
 
 
 def solution(mesh):

time: 90.1 us -> 78.4 us (0.87)
  local copies, waits for them, and re-layouts: 12.4 us -> 2.81 us
  Pallas kernels: 76.7 us -> 74.8 us
    unnamed x3 -> x2, local copies, waits for them, and re-layouts: 10.9 us -> 2.81 us
    pallas_call x1, Pallas kernels: 76.7 us -> 74.8 us  [body(): pl.pallas_call(kernel, out_shape=(jax.ShapeDtypeStruct((2, 8, D), f32), j...]
where the time goes in v2:
time: 78.4 us; the launch traced here: 78.2 us
  Pallas kernels  74.8 us (95%)
  local copies, waits for them, and re-layouts  2.81 us (4%)
    pallas_call x1, Pallas kernels, body(): pl.pallas_call(kernel, out_shape=(jax.ShapeDtypeStruct((2, 8, D), f32), j...  74.8 us
    unnamed x2, local copies, waits for them, and re-layouts  2.81 us

profile of v2, /device:TPU:0, one launch (start us, length us, event | category | flops | bytes accessed | tf_op | source)
XLA Modules:
  0.0 78.2 jit_solution(17966428961326929749)
XLA Ops:
  0.6 74.8 %latent_attention.1 = (f32[2,8,2304]{2,1,0:T(8,128)}, f32[1,512]{1,0:T(1,128)}) custom-call(f32[2,8,2304]{2,1,0:T(8,128)} %bitcast.8, s32[16,128]{1,0:T(8,128)} %bitcast.9, f32[192,2304]{1,0:T(8,128)} %bitcast.6, f32[576,2304]{1,0:T(8,128)} %bitcast.5, f32[512,256]{1,0:T(8,128)} %wu_in.1, f32[128,2304]{1,0:T(8,128)} %wo_in.1), custom_call_target="tpu_custom_call" | custom-call | tf_op jit(solution)/shard_map/latent_attention/pallas_call | solution.py:370
  75.4 1.6 %copy.10 = f32[16,2304]{1,0:T(8,128)} copy(f32[16,2304]{1,0:T(8,128)} %bitcast.7) | data formatting | bytes 294912
  77.0 1.2 %copy.11 = f32[1,512]{1,0:T(1,128)} copy(f32[1,512]{1,0:T(1,128)} %get-tuple-element.9) | data formatting | bytes 4096

commit v3 on v2

--- a/solution.py
+++ b/solution.py
@@ -23,7 +23,7 @@
 f32 = jnp.float32
 bf16 = jnp.bfloat16
 MESH = pl.DeviceIdType.MESH
-N_SEM = 160
+N_SEM = 200
 
 
 def split(value):
@@ -44,7 +44,7 @@
 def kernel(
     x_in, seg_in, wq_in, wd_in, wu_in, wo_in,
     out, ln_out,
-    xs, lat, wq, wd, wu, wo, kv, kv_far, qh, ql, accq,
+    xs, lat, wq, wd, wu, wo, wqh, wql, wuh, wul, woh, wol, kv, kv_far, qh, ql, accq,
     top, tot, acc, part, relay, sums, sums2, red, ln, ln_far,
     send_sem, recv_sem, load_sem,
 ):
@@ -66,10 +66,10 @@
     Z_UP, Z_DOWN = at(y0, zp), at(y0, zm)
     Y_OPP, Z_OPP = at(yo, z0), at(y0, zo)
     PARTNER = (ctx, head + 1 - 2 * core)
-    X_PEERS = [(turn(ctx, by), head) for by in (1, 2, 3)]
+    X_UP, X_DOWN, X_OPP = [(turn(ctx, by), head) for by in (1, -1, 2)]
 
     barrier = pltpu.get_barrier_semaphore()
-    peers = [Y_UP, Y_DOWN, Z_UP, Z_DOWN, Y_OPP, Z_OPP, PARTNER] + X_PEERS
+    peers = [Y_UP, Y_DOWN, Z_UP, Z_DOWN, Y_OPP, Z_OPP, PARTNER, X_UP, X_DOWN, X_OPP]
     for peer in peers:
         pl.semaphore_signal(barrier, inc=1, device_id=peer, device_id_type=MESH)
 
@@ -91,8 +91,6 @@
     load_rest = [
         load(wq_in, wq.at[core]), load(wu_in, wu.at[core]), load(wo_in, wo.at[core])
     ]
-    pl.semaphore_wait(barrier, len(peers))
-
     copies = []
 
     def send(src, dst, device):
@@ -148,18 +146,51 @@
         cols = everything if p is None else pl.ds(p * HALF, HALF)
         return xs.at[y, z, :, :, cols] if h is None else xs.at[y, z, h, :, cols]
 
-    def lat_view(y, z, p, h):
-        return lat.at[y, z, everything if p is None else p, everything if h is None else h]
+    def gather_small(slot, neighbours=False):
+        def whole(y, z):
+            return lat.at[y, z, slot]
+
+        def some(y, z, p):
+            return lat.at[y, z, slot, (pl.ds(0, 4), pl.ds(4, 5))[p]]
+
+        passed = {}
+
+        def pass_on(y, z, name):
+            if neighbours:
+                passed[name] = (
+                    send(whole(y, z), lat.at[y, z, 2], X_UP),
+                    send(whole(y, z), lat.at[y, z, 3], X_DOWN),
+                )
+
+        to_y, to_z = (Y_UP, Y_DOWN, Y_OPP), (Z_UP, Z_DOWN, Z_OPP)
+        from_y, from_z = (ym, yp, yo), (zm, zp, zo)
+        on_y, on_z = [], []
+        for k in range(3):
+            on_y.append(send(whole(y0, z0), whole(y0, z0), to_y[k]))
+            on_z.append(send(whole(y0, z0), whole(y0, z0), to_z[k]))
+        pass_on(y0, z0, "own")
+        yield passed
+        a, b = {}, {}
+        for k in range(3):
+            on_y[k].wait_recv()
+            for j in range(3):
+                a[k, j] = send(some(from_y[k], z0, 0), some(from_y[k], z0, 0), to_z[j])
+            on_z[k].wait_recv()
+            for j in range(3):
+                b[j, k] = send(some(y0, from_z[k], 1), some(y0, from_z[k], 1), to_y[j])
+            pass_on(from_y[k], z0, ("y", k))
+            pass_on(y0, from_z[k], ("z", k))
+        yield passed
+        for j in range(3):
+            for k in range(3):
+                a[k, j].wait_recv()
+                b[k, j].wait_recv()
+                pass_on(from_y[k], from_z[j], (k, j))
+        yield passed
 
     gather_x = gather(x_view, x_in)
-    next(gather_x)
+
     load_x.wait()
-    weight_copies = [
-        send(wq_in, wq.at[core], PARTNER),
-        send(wu_in, wu.at[core], PARTNER),
-        send(wo_in, wo.at[core], PARTNER),
-    ]
-
     own_high, own_low = split(xs[y0, z0].reshape(16, D))
     own_both = jnp.concatenate([own_high, own_low], axis=0)
     raw2 = jnp.zeros((32, KV_RANK + ROPE), f32)
@@ -171,45 +202,52 @@
         raw2 = raw2 + dot(own_both[:, cols], w_high, ((1,), (1,)))
         raw1 = raw1 + dot(own_high[:, cols], w_low, ((1,), (1,)))
         if i == 0:
+            pl.semaphore_wait(barrier, len(peers))
             next(gather_x)
+            weight_copies = [
+                send(wq_in, wq.at[core], PARTNER),
+                send(wu_in, wu.at[core], PARTNER),
+                send(wo_in, wo.at[core], PARTNER),
+            ]
     raw = raw2[:16] + (raw2[16:] + raw1)
     squeezed = raw[:, :KV_RANK]
     mean_square = jnp.mean(squeezed * squeezed, axis=1, keepdims=True)
-    c_hi, c_lo = lax.div(ctx, 2), lax.rem(ctx, 2)
     squeezed = squeezed * lax.rsqrt(mean_square + eps_norm)
     for j in range(4):
         tiles = squeezed[:, j * 128 : (j + 1) * 128].reshape(2, 8, 128)
-        lat[y0, z0, c_hi, c_lo, pl.ds(2 * j, 2)] = tiles
-    lat[y0, z0, c_hi, c_lo, 8] = jnp.concatenate([raw[:8, KV_RANK:], raw[8:, KV_RANK:]], axis=1)
-    own_lat = lat.at[y0, z0, c_hi, c_lo]
-    across = [send(own_lat, own_lat, peer) for peer in X_PEERS]
+        lat[y0, z0, 0, pl.ds(2 * j, 2)] = tiles
+    lat[y0, z0, 0, 8] = jnp.concatenate([raw[:8, KV_RANK:], raw[8:, KV_RANK:]], axis=1)
+
+    across = send(lat.at[y0, z0, 0], lat.at[y0, z0, 1], X_OPP)
+    gather_own = gather_small(0, neighbours=True)
+    gather_opp = gather_small(1)
+    passed = next(gather_own)
     next(gather_x)
-    for copy in across:
-        copy.wait_recv()
-    gather_lat = gather(lat_view)
-    next(gather_lat)
+    next(gather_own)
     next(gather_x)
-    next(gather_lat)
-    next(gather_x)
-    next(gather_lat)
-
+    across.wait_recv()
+    next(gather_opp)
     for copy in load_rest:
         copy.wait()
     for copy in weight_copies:
         copy.wait_recv()
+    for h in range(2):
+        wqh[h], wql[h] = split(wq[h])
+        wuh[h], wul[h] = split(wu[h])
+    next(gather_own)
+    next(gather_x)
+    next(gather_opp)
+    woh[...], wol[...] = split(wo[...].reshape(2 * VDIM, D))
+    next(gather_x)
 
     accq[...] = jnp.zeros_like(accq)
 
-    def query_columns(k, carry):
+    @pl.loop(0, D // 256)
+    def _(k):
         cols = pl.ds(pl.multiple_of(k * 256, 256), 256)
         rows = split(xs[:, :, :, :, cols].reshape(256, 256))
         for h in range(2):
-            accq[h] += dot3(rows, split(wq[h, :, cols]), ((1,), (1,)))
-        return carry
-
-    lax.fori_loop(0, 4, query_columns, 0)
-    next(gather_lat)
-    lax.fori_loop(4, D // 256, query_columns, 0)
+            accq[h] += dot3(rows, (wqh[h, :, cols], wql[h, :, cols]), ((1,), (1,)))
 
     for h in range(2):
         qh[h], ql[h] = split(accq[h] * (1.0 / math.sqrt(QK)))
@@ -219,17 +257,15 @@
     lane = lax.broadcasted_iota(jnp.int32, (1, 256), 1)
     q_pos = ctx * TOK_CTX + lax.div(lane, 16) * 32 + core * 16 + lax.rem(lane, 16)
     q_start = jnp.where(q_pos >= bound, bound, 0)
-    row = lax.broadcasted_iota(jnp.int32, (128, 1), 0)
-    row_block, row_ctx, row_in = lax.div(row, 32), lax.rem(lax.div(row, 16), 2), lax.rem(row, 16)
+    row = lax.broadcasted_iota(jnp.int32, (256, 1), 0)
+    row_in, row_block = lax.rem(row, 16), lax.div(row, 16)
+    slot_ctx = (ctx, turn(ctx, 2), turn(ctx, -1), turn(ctx, 1))
 
     top[...] = jnp.full_like(top, neg_fill)
     tot[...] = jnp.zeros_like(tot)
     acc[...] = jnp.zeros_like(acc)
 
-    def attend(block, y, z, side):
-        pos_a = row_ctx * TOK_CTX + (row_block * 4 + z) * 32 + row_in + side * 16
-        pos_b = (row_ctx + 2) * TOK_CTX + (y * 4 + row_block) * 32 + row_in + side * 16
-        k_pos = jnp.concatenate([pos_a, pos_b], axis=0)
+    def attend(block, k_pos):
         allowed = (k_pos <= q_pos) & (k_pos >= q_start)
         for h in range(2):
             keys = jnp.concatenate(
@@ -239,41 +275,57 @@
             scores = jnp.where(allowed, scores, neg_fill)
             old = top[h]
             new = jnp.maximum(old, jnp.max(scores, axis=0, keepdims=True))
-            weights = jnp.where(allowed, jnp.exp(scores - new), 0.0)
+            weights = jnp.exp(scores - new)
             factor = jnp.exp(old - new)
             top[h] = new
             tot[h] = tot[h] * factor + jnp.sum(weights, axis=0, keepdims=True)
             values = block[:, h * 256 + NOPE : (h + 1) * 256].T
             acc[h] = acc[h] * factor + dot3(split(values), split(weights))
 
-    def make(g, y, z):
+    def make(g, pieces):
         def columns(tiles):
-            pair = [lat[:, z, 0, :, tiles], lat[y, :, 1, :, tiles]]
-            return jnp.concatenate([value.reshape(-1, 128) for value in pair], axis=0)
+            taken = [
+                lat[:, :, slot, tiles] if z is None else lat[:, z, slot, tiles]
+                for slot, z in pieces
+            ]
+            return jnp.concatenate([value.reshape(-1, 128) for value in taken], axis=0)
 
         both = split(jnp.concatenate([columns(pl.ds(2 * j, 2)) for j in range(4)], axis=1))
         for h in range(2):
-            kv[g, :, pl.ds(h * 256, 256)] = dot3(both, split(wu[h]))
+            kv[g, :, pl.ds(h * 256, 256)] = dot3(both, (wuh[h], wul[h]))
         shared = columns(8).reshape(16, 8, 128)
         shared = jnp.concatenate([shared[:, :, :64], shared[:, :, 64:]], axis=1).reshape(256, 64)
         kv[g, :, pl.ds(512, 64)] = shared
         kv[g, :, pl.ds(576, 64)] = jnp.zeros((256, 64), f32)
         return send(kv.at[g], kv_far.at[g], PARTNER)
 
-    first = make(0, y0, z0)
-    attend(kv[0], y0, z0, core)
-    first.wait_recv()
-    attend(kv_far[0], y0, z0, 1 - core)
-    steps = [make(1, ym, zm), make(2, yp, zp)]
-    for g, (y, z) in ((1, (ym, zm)), (2, (yp, zp))):
-        attend(kv[g], y, z, core)
-        steps[g - 1].wait_recv()
-        attend(kv_far[g], y, z, 1 - core)
-    next(gather_lat)
-    final = make(3, yo, zo)
-    attend(kv[3], yo, zo, core)
-    final.wait_recv()
-    attend(kv_far[3], yo, zo, 1 - core)
+    def chunk(g, pieces):
+        copy = make(g, pieces)
+        if len(pieces) == 1:
+            at_ctx, block = slot_ctx[pieces[0][0]], row_block
+        else:
+            pick = lax.div(row, 64)
+            at_ctx = jnp.where(pick < 2, slot_ctx[2], slot_ctx[3])
+            column = jnp.where(lax.rem(pick, 2) == 0, pieces[0][1], pieces[1][1])
+            block = lax.rem(row_block, 4) * 4 + column
+        k_pos = at_ctx * TOK_CTX + block * 32 + row_in
+        attend(kv[g], k_pos + core * 16)
+        copy.wait_recv()
+        attend(kv_far[g], k_pos + (1 - core) * 16)
+
+    chunk(0, [(0, None)])
+    next(gather_opp)
+    chunk(1, [(1, None)])
+    names = ["own", ("y", 0), ("y", 1), ("y", 2)], [("z", 0), (0, 0), (1, 0), (2, 0)]
+    for name in (*names[0], *names[1]):
+        for copy in passed[name]:
+            copy.wait_recv()
+    chunk(2, [(2, z0), (2, zm), (3, z0), (3, zm)])
+    for j in (1, 2):
+        for name in (("z", j), (0, j), (1, j), (2, j)):
+            for copy in passed[name]:
+                copy.wait_recv()
+    chunk(3, [(2, zp), (2, zo), (3, zp), (3, zo)])
 
     heads = []
     for h in range(2):
@@ -301,8 +353,7 @@
         tile = HALF // 3
         for t in range(3):
             cols = pl.ds(p * HALF + t * tile, tile)
-            w_out = split(wo[:, :, cols].reshape(256, tile))
-            part[:, :, :, :, cols] = dot3(rows, w_out).reshape(4, 4, 2, 8, tile)
+            part[:, :, :, :, cols] = dot3(rows, (woh[:, cols], wol[:, cols])).reshape(4, 4, 2, 8, tile)
         for i in range(4):
             relays[p, i] = (
                 send(rows_of(p, uo, i, 0), relay.at[p, 0, i], upward),
@@ -377,11 +428,17 @@
         out_specs=(vmem, vmem),
         scratch_shapes=[
             pltpu.VMEM((4, 4, 2, 8, D), f32),
-            pltpu.VMEM((4, 4, 2, 2, 9, 8, 128), f32),
+            pltpu.VMEM((4, 4, 4, 9, 8, 128), f32),
             pltpu.VMEM((2, QK, D), f32),
             pltpu.VMEM((KV_RANK + ROPE, D), f32),
             pltpu.VMEM((2, KV_RANK, 256), f32),
             pltpu.VMEM((2, VDIM, D), f32),
+            pltpu.VMEM((2, QK, D), bf16),
+            pltpu.VMEM((2, QK, D), bf16),
+            pltpu.VMEM((2, KV_RANK, 256), bf16),
+            pltpu.VMEM((2, KV_RANK, 256), bf16),
+            pltpu.VMEM((2 * VDIM, D), bf16),
+            pltpu.VMEM((2 * VDIM, D), bf16),
             pltpu.VMEM((4, 256, LAT), f32),
             pltpu.VMEM((4, 256, LAT), f32),
             pltpu.VMEM((2, 256, QK), bf16),

time: 78.4 us -> 75.7 us (0.966)
  Pallas kernels: 74.8 us -> 72.1 us
    pallas_call x1, Pallas kernels: 74.8 us -> 72.1 us  [body(): pl.pallas_call(kernel, out_shape=(jax.ShapeDtypeStruct((2, 8, D), f32), j...]
where the time goes in v3:
time: 75.7 us; the launch traced here: 75.5 us
  Pallas kernels  72.1 us (95%)
  local copies, waits for them, and re-layouts  2.81 us (4%)
    pallas_call x1, Pallas kernels, body(): pl.pallas_call(kernel, out_shape=(jax.ShapeDtypeStruct((2, 8, D), f32), j...  72.1 us
    unnamed x2, local copies, waits for them, and re-layouts  2.81 us

profile of v3, /device:TPU:0, one launch (start us, length us, event | category | flops | bytes accessed | tf_op | source)
XLA Modules:
  0.0 75.5 jit_solution(10000904046635123939)
XLA Ops:
  0.6 72.1 %latent_attention.1 = (f32[2,8,2304]{2,1,0:T(8,128)}, f32[1,512]{1,0:T(1,128)}) custom-call(f32[2,8,2304]{2,1,0:T(8,128)} %bitcast.8, s32[16,128]{1,0:T(8,128)} %bitcast.9, f32[192,2304]{1,0:T(8,128)} %bitcast.6, f32[576,2304]{1,0:T(8,128)} %bitcast.5, f32[512,256]{1,0:T(8,128)} %wu_in.1, f32[128,2304]{1,0:T(8,128)} %wo_in.1), custom_call_target="tpu_custom_call" | custom-call | tf_op jit(solution)/shard_map/latent_attention/pallas_call | solution.py:421
  72.7 1.6 %copy.10 = f32[16,2304]{1,0:T(8,128)} copy(f32[16,2304]{1,0:T(8,128)} %bitcast.7) | data formatting | bytes 294912
  74.3 1.2 %copy.11 = f32[1,512]{1,0:T(1,128)} copy(f32[1,512]{1,0:T(1,128)} %get-tuple-element.9) | data formatting | bytes 4096

commit v4 on v3

--- a/solution.py
+++ b/solution.py
@@ -45,7 +45,7 @@
     x_in, seg_in, wq_in, wd_in, wu_in, wo_in,
     out, ln_out,
     xs, lat, wq, wd, wu, wo, wqh, wql, wuh, wul, woh, wol, kv, kv_far, qh, ql, accq,
-    top, tot, acc, part, relay, sums, sums2, red, ln, ln_far,
+    top, tot, acc, part, relay, sums, sums2, red, ln, ln_far, seg, ln_row, rows_out,
     send_sem, recv_sem, load_sem,
 ):
     ctx = lax.axis_index("ctx")
@@ -89,7 +89,8 @@
         for i in range(WD_STEPS)
     ]
     load_rest = [
-        load(wq_in, wq.at[core]), load(wu_in, wu.at[core]), load(wo_in, wo.at[core])
+        load(wq_in, wq.at[core]), load(wu_in, wu.at[core]), load(wo_in, wo.at[core]),
+        load(seg_in, seg),
     ]
     copies = []
 
@@ -188,6 +189,23 @@
                 pass_on(from_y[k], from_z[j], (k, j))
         yield passed
 
+    def make(g, pieces):
+        def columns(tiles):
+            taken = [
+                lat[:, :, slot, tiles] if z is None else lat[:, z, slot, tiles]
+                for slot, z in pieces
+            ]
+            return jnp.concatenate([value.reshape(-1, 128) for value in taken], axis=0)
+
+        both = split(jnp.concatenate([columns(pl.ds(2 * j, 2)) for j in range(4)], axis=1))
+        for h in range(2):
+            kv[g, :, pl.ds(h * 256, 256)] = dot3(both, (wuh[h], wul[h]))
+        shared = columns(8).reshape(16, 8, 128)
+        shared = jnp.concatenate([shared[:, :, :64], shared[:, :, 64:]], axis=1).reshape(256, 64)
+        kv[g, :, pl.ds(512, 64)] = shared
+        kv[g, :, pl.ds(576, 64)] = jnp.zeros((256, 64), f32)
+        return send(kv.at[g], kv_far.at[g], PARTNER)
+
     gather_x = gather(x_view, x_in)
 
     load_x.wait()
@@ -222,20 +240,22 @@
     gather_own = gather_small(0, neighbours=True)
     gather_opp = gather_small(1)
     passed = next(gather_own)
-    next(gather_x)
-    next(gather_own)
-    next(gather_x)
-    across.wait_recv()
-    next(gather_opp)
     for copy in load_rest:
         copy.wait()
     for copy in weight_copies:
         copy.wait_recv()
     for h in range(2):
         wqh[h], wql[h] = split(wq[h])
-        wuh[h], wul[h] = split(wu[h])
+    next(gather_x)
+    next(gather_x)
     next(gather_own)
     next(gather_x)
+    for h in range(2):
+        wuh[h], wul[h] = split(wu[h])
+    across.wait_recv()
+    next(gather_opp)
+    next(gather_own)
+    made = {0: make(0, [(0, None)])}
     next(gather_opp)
     woh[...], wol[...] = split(wo[...].reshape(2 * VDIM, D))
     next(gather_x)
@@ -252,7 +272,7 @@
     for h in range(2):
         qh[h], ql[h] = split(accq[h] * (1.0 / math.sqrt(QK)))
 
-    ones = jnp.sum(seg_in[...], axis=(0, 1), keepdims=True)
+    ones = jnp.sum(seg[...], axis=(0, 1), keepdims=True)
     bound = 2048 - ones
     lane = lax.broadcasted_iota(jnp.int32, (1, 256), 1)
     q_pos = ctx * TOK_CTX + lax.div(lane, 16) * 32 + core * 16 + lax.rem(lane, 16)
@@ -282,25 +302,7 @@
             values = block[:, h * 256 + NOPE : (h + 1) * 256].T
             acc[h] = acc[h] * factor + dot3(split(values), split(weights))
 
-    def make(g, pieces):
-        def columns(tiles):
-            taken = [
-                lat[:, :, slot, tiles] if z is None else lat[:, z, slot, tiles]
-                for slot, z in pieces
-            ]
-            return jnp.concatenate([value.reshape(-1, 128) for value in taken], axis=0)
-
-        both = split(jnp.concatenate([columns(pl.ds(2 * j, 2)) for j in range(4)], axis=1))
-        for h in range(2):
-            kv[g, :, pl.ds(h * 256, 256)] = dot3(both, (wuh[h], wul[h]))
-        shared = columns(8).reshape(16, 8, 128)
-        shared = jnp.concatenate([shared[:, :, :64], shared[:, :, 64:]], axis=1).reshape(256, 64)
-        kv[g, :, pl.ds(512, 64)] = shared
-        kv[g, :, pl.ds(576, 64)] = jnp.zeros((256, 64), f32)
-        return send(kv.at[g], kv_far.at[g], PARTNER)
-
-    def chunk(g, pieces):
-        copy = make(g, pieces)
+    def positions(pieces):
         if len(pieces) == 1:
             at_ctx, block = slot_ctx[pieces[0][0]], row_block
         else:
@@ -308,24 +310,39 @@
             at_ctx = jnp.where(pick < 2, slot_ctx[2], slot_ctx[3])
             column = jnp.where(lax.rem(pick, 2) == 0, pieces[0][1], pieces[1][1])
             block = lax.rem(row_block, 4) * 4 + column
-        k_pos = at_ctx * TOK_CTX + block * 32 + row_in
-        attend(kv[g], k_pos + core * 16)
-        copy.wait_recv()
-        attend(kv_far[g], k_pos + (1 - core) * 16)
-
-    chunk(0, [(0, None)])
-    next(gather_opp)
-    chunk(1, [(1, None)])
-    names = ["own", ("y", 0), ("y", 1), ("y", 2)], [("z", 0), (0, 0), (1, 0), (2, 0)]
-    for name in (*names[0], *names[1]):
-        for copy in passed[name]:
-            copy.wait_recv()
-    chunk(2, [(2, z0), (2, zm), (3, z0), (3, zm)])
-    for j in (1, 2):
-        for name in (("z", j), (0, j), (1, j), (2, j)):
+        return at_ctx * TOK_CTX + block * 32 + row_in
+
+    def arrive(names):
+        for name in names:
             for copy in passed[name]:
                 copy.wait_recv()
-    chunk(3, [(2, zp), (2, zo), (3, zp), (3, zo)])
+
+    chunks = (
+        [(0, None)],
+        [(1, None)],
+        [(2, z0), (2, zm), (3, z0), (3, zm)],
+        [(2, zp), (2, zo), (3, zp), (3, zo)],
+    )
+    near = ["own", ("y", 0), ("y", 1), ("y", 2), ("z", 0), (0, 0), (1, 0), (2, 0)]
+    far = [(name, j) for j in (1, 2) for name in ("z", 0, 1, 2)]
+    attend(kv[0], positions(chunks[0]) + core * 16)
+    next(gather_opp)
+    made[1] = make(1, chunks[1])
+    made[0].wait_recv()
+    attend(kv_far[0], positions(chunks[0]) + (1 - core) * 16)
+    attend(kv[1], positions(chunks[1]) + core * 16)
+    arrive(near)
+    made[2] = make(2, chunks[2])
+    made[1].wait_recv()
+    attend(kv_far[1], positions(chunks[1]) + (1 - core) * 16)
+    attend(kv[2], positions(chunks[2]) + core * 16)
+    arrive(far)
+    made[3] = make(3, chunks[3])
+    made[2].wait_recv()
+    attend(kv_far[2], positions(chunks[2]) + (1 - core) * 16)
+    attend(kv[3], positions(chunks[3]) + core * 16)
+    made[3].wait_recv()
+    attend(kv_far[3], positions(chunks[3]) + (1 - core) * 16)
 
     heads = []
     for h in range(2):
@@ -404,28 +421,32 @@
         middle = rest.astype(bf16)
         lowest = (rest - middle.astype(f32)).astype(bf16)
         placed = placed + ((dot(high, place) + dot(middle, place)) + dot(lowest, place))
-    ln_out[...] = placed[:1]
+    ln_row[...] = placed[:1]
+    stores = [load(ln_row, ln_out)]
 
     for p in range(2):
         for i in range(3):
             final2[p, i].wait_recv()
         total = red[p, 3] + sums2[p, 0] + (sums2[p, 1] + sums2[p, 2])
-        out[:, :, pl.ds(p * HALF, HALF)] = total
+        rows_out[:, :, pl.ds(p * HALF, HALF)] = total
+        cols = pl.ds(p * HALF, HALF)
+        stores.append(load(rows_out.at[:, :, cols], out.at[:, :, cols]))
+    for copy in stores:
+        copy.wait()
     for copy in copies:
         copy.wait_send()
 
 
 def body(hidden_rows, segment_ids, w_query, w_down, w_up, w_out):
     any_space = pl.BlockSpec(memory_space=pl.ANY)
-    vmem = pl.BlockSpec(memory_space=pltpu.VMEM)
     out, ln = pl.pallas_call(
         kernel,
         out_shape=(
             jax.ShapeDtypeStruct((2, 8, D), f32),
             jax.ShapeDtypeStruct((1, TOK_CTX), f32),
         ),
-        in_specs=[any_space, vmem, any_space, any_space, any_space, any_space],
-        out_specs=(vmem, vmem),
+        in_specs=[any_space] * 6,
+        out_specs=(any_space, any_space),
         scratch_shapes=[
             pltpu.VMEM((4, 4, 2, 8, D), f32),
             pltpu.VMEM((4, 4, 4, 9, 8, 128), f32),
@@ -454,9 +475,12 @@
             pltpu.VMEM((2, 4, 2, 8, HALF), f32),
             pltpu.VMEM((2, 8, 256), f32),
             pltpu.VMEM((8, 256), f32),
+            pltpu.VMEM((16, 128), jnp.int32),
+            pltpu.VMEM((1, TOK_CTX), f32),
+            pltpu.VMEM((2, 8, D), f32),
             pltpu.SemaphoreType.DMA((N_SEM,)),
             pltpu.SemaphoreType.DMA((N_SEM,)),
-            pltpu.SemaphoreType.DMA((8,)),
+            pltpu.SemaphoreType.DMA((16,)),
         ],
         compiler_params=pltpu.CompilerParams(
             collective_id=0, has_side_effects=True, vmem_limit_bytes=58 * 1024 * 1024

time: 75.7 us -> 70 us (0.925)
  Pallas kernels: 72.1 us -> 66.4 us
    pallas_call x1, Pallas kernels: 72.1 us -> 66.4 us  [body(): pl.pallas_call(kernel, out_shape=(jax.ShapeDtypeStruct((2, 8, D), f32), j...]
where the time goes in v4:
time: 70 us; the launch traced here: 69.8 us
  Pallas kernels  66.4 us (95%)
  local copies, waits for them, and re-layouts  2.81 us (4%)
    pallas_call x1, Pallas kernels, body(): pl.pallas_call(kernel, out_shape=(jax.ShapeDtypeStruct((2, 8, D), f32), j...  66.4 us
    unnamed x2, local copies, waits for them, and re-layouts  2.81 us

profile of v4, /device:TPU:0, one launch (start us, length us, event | category | flops | bytes accessed | tf_op | source)
XLA Modules:
  0.0 69.8 jit_solution(6851990795965001887)
XLA Ops:
  0.6 66.4 %latent_attention.1 = (f32[2,8,2304]{2,1,0:T(8,128)}, f32[1,512]{1,0:T(1,128)}) custom-call(f32[2,8,2304]{2,1,0:T(8,128)} %bitcast.8, s32[16,128]{1,0:T(8,128)} %bitcast.9, f32[192,2304]{1,0:T(8,128)} %bitcast.6, f32[576,2304]{1,0:T(8,128)} %bitcast.5, f32[512,256]{1,0:T(8,128)} %wu_in.1, f32[128,2304]{1,0:T(8,128)} %wo_in.1), custom_call_target="tpu_custom_call" | custom-call | tf_op jit(solution)/shard_map/latent_attention/pallas_call | solution.py:442
  67.0 1.6 %copy.10 = f32[16,2304]{1,0:T(8,128)} copy(f32[16,2304]{1,0:T(8,128)} %bitcast.7) | data formatting | bytes 294912
  68.6 1.2 %copy.11 = f32[1,512]{1,0:T(1,128)} copy(f32[1,512]{1,0:T(1,128)} %get-tuple-element.9) | data formatting | bytes 4096

commit v5 on v4

--- a/solution.py
+++ b/solution.py
@@ -45,7 +45,7 @@
     x_in, seg_in, wq_in, wd_in, wu_in, wo_in,
     out, ln_out,
     xs, lat, wq, wd, wu, wo, wqh, wql, wuh, wul, woh, wol, kv, kv_far, qh, ql, accq,
-    top, tot, acc, part, relay, sums, sums2, red, ln, ln_far, seg, ln_row, rows_out,
+    top, tot, acc, part, relay, sums, sums2, red, ln, ln_far, seg, ln_row, rows_out, xh, xl,
     send_sem, recv_sem, load_sem,
 ):
     ctx = lax.axis_index("ctx")
@@ -261,13 +261,9 @@
     next(gather_x)
 
     accq[...] = jnp.zeros_like(accq)
-
-    @pl.loop(0, D // 256)
-    def _(k):
-        cols = pl.ds(pl.multiple_of(k * 256, 256), 256)
-        rows = split(xs[:, :, :, :, cols].reshape(256, 256))
-        for h in range(2):
-            accq[h] += dot3(rows, (wqh[h, :, cols], wql[h, :, cols]), ((1,), (1,)))
+    xh[...], xl[...] = split(xs[...].reshape(256, D))
+    for h in range(2):
+        accq[h] = dot3((xh[...], xl[...]), (wqh[h], wql[h]), ((1,), (1,)))
 
     for h in range(2):
         qh[h], ql[h] = split(accq[h] * (1.0 / math.sqrt(QK)))
@@ -287,20 +283,24 @@
 
     def attend(block, k_pos):
         allowed = (k_pos <= q_pos) & (k_pos >= q_start)
+        found, stats = [], []
         for h in range(2):
             keys = jnp.concatenate(
                 [block[:, h * 256 : h * 256 + NOPE], block[:, 512 : 512 + ROPE]], axis=1
             )
             scores = dot3(split(keys), (qh[h], ql[h]), ((1,), (1,)))
-            scores = jnp.where(allowed, scores, neg_fill)
+            found.append(jnp.where(allowed, scores, neg_fill))
+        for h in range(2):
             old = top[h]
-            new = jnp.maximum(old, jnp.max(scores, axis=0, keepdims=True))
-            weights = jnp.exp(scores - new)
+            new = jnp.maximum(old, jnp.max(found[h], axis=0, keepdims=True))
+            weights = jnp.exp(found[h] - new)
             factor = jnp.exp(old - new)
             top[h] = new
             tot[h] = tot[h] * factor + jnp.sum(weights, axis=0, keepdims=True)
-            values = block[:, h * 256 + NOPE : (h + 1) * 256].T
-            acc[h] = acc[h] * factor + dot3(split(values), split(weights))
+            stats.append((factor, split(weights)))
+        for h in range(2):
+            values = split(block[:, h * 256 + NOPE : (h + 1) * 256].T)
+            acc[h] = acc[h] * stats[h][0] + dot3(values, stats[h][1])
 
     def positions(pieces):
         if len(pieces) == 1:
@@ -365,6 +365,14 @@
         return part.at[v, u, h, :, cols] if p == 0 else part.at[u, v, h, :, cols]
 
     relays, direct, second, final2 = {}, {}, {}, {}
+
+    def send_direct(p, i):
+        (um, u0, up, uo), down, upward, _ = axes[p]
+        direct[p, i] = (
+            send(rows_of(p, up, i, 1), sums.at[p, 0, i, 1], upward),
+            send(rows_of(p, um, i, 0), sums.at[p, 1, i, 0], down),
+        )
+
     for p in range(2):
         (um, u0, up, uo), down, upward, _ = axes[p]
         tile = HALF // 3
@@ -376,11 +384,8 @@
                 send(rows_of(p, uo, i, 0), relay.at[p, 0, i], upward),
                 send(rows_of(p, uo, i, 1), relay.at[p, 1, i], down),
             )
-        for i in range(4):
-            direct[p, i] = (
-                send(rows_of(p, up, i, 1), sums.at[p, 0, i, 1], upward),
-                send(rows_of(p, um, i, 0), sums.at[p, 1, i, 0], down),
-            )
+        for i in range(2):
+            send_direct(p, i)
 
     def pass_on(p, i):
         (um, u0, up, uo), down, upward, _ = axes[p]
@@ -402,12 +407,14 @@
             device = (opposite, down, upward)[i]
             final2[p, i] = send(red.at[p, i], sums2.at[p, i], device)
 
-    for stage in range(6):
+    for i in range(4):
         for p in range(2):
-            if stage < 4:
-                pass_on(p, stage)
-            if stage >= 2:
-                finish(p, stage - 2)
+            pass_on(p, i)
+            if i < 2:
+                send_direct(p, i + 2)
+    for i in range(4):
+        for p in range(2):
+            finish(p, i)
 
     ln_copy.wait_recv()
     from_lane = lax.broadcasted_iota(jnp.int32, (256, 512), 0)
@@ -478,6 +485,8 @@
             pltpu.VMEM((16, 128), jnp.int32),
             pltpu.VMEM((1, TOK_CTX), f32),
             pltpu.VMEM((2, 8, D), f32),
+            pltpu.VMEM((256, D), bf16),
+            pltpu.VMEM((256, D), bf16),
             pltpu.SemaphoreType.DMA((N_SEM,)),
             pltpu.SemaphoreType.DMA((N_SEM,)),
             pltpu.SemaphoreType.DMA((16,)),

time: 70 us -> 65.9 us (0.941)
  Pallas kernels: 66.4 us -> 62.3 us
    pallas_call x1, Pallas kernels: 66.4 us -> 62.3 us  [body(): pl.pallas_call(kernel, out_shape=(jax.ShapeDtypeStruct((2, 8, D), f32), j...]
where the time goes in v5:
time: 65.9 us; the launch traced here: 65.7 us
  Pallas kernels  62.3 us (95%)
  local copies, waits for them, and re-layouts  2.81 us (4%)
    pallas_call x1, Pallas kernels, body(): pl.pallas_call(kernel, out_shape=(jax.ShapeDtypeStruct((2, 8, D), f32), j...  62.3 us
    unnamed x2, local copies, waits for them, and re-layouts  2.81 us

profile of v5, /device:TPU:0, one launch (start us, length us, event | category | flops | bytes accessed | tf_op | source)
XLA Modules:
  0.0 65.7 jit_solution(13698143556513066638)
XLA Ops:
  0.6 62.3 %latent_attention.1 = (f32[2,8,2304]{2,1,0:T(8,128)}, f32[1,512]{1,0:T(1,128)}) custom-call(f32[2,8,2304]{2,1,0:T(8,128)} %bitcast.8, s32[16,128]{1,0:T(8,128)} %bitcast.9, f32[192,2304]{1,0:T(8,128)} %bitcast.6, f32[576,2304]{1,0:T(8,128)} %bitcast.5, f32[512,256]{1,0:T(8,128)} %wu_in.1, f32[128,2304]{1,0:T(8,128)} %wo_in.1), custom_call_target="tpu_custom_call" | custom-call | tf_op jit(solution)/shard_map/latent_attention/pallas_call | solution.py:449
  62.9 1.6 %copy.10 = f32[16,2304]{1,0:T(8,128)} copy(f32[16,2304]{1,0:T(8,128)} %bitcast.7) | data formatting | bytes 294912
  64.5 1.2 %copy.11 = f32[1,512]{1,0:T(1,128)} copy(f32[1,512]{1,0:T(1,128)} %get-tuple-element.9) | data formatting | bytes 4096

commit v6 on v5

--- a/solution.py
+++ b/solution.py
@@ -82,7 +82,7 @@
         return copy
 
     load_x = load(x_in, xs.at[y0, z0])
-    WD_STEPS = 3
+    WD_STEPS = 6
     wd_rows = D // WD_STEPS
     load_wd = [
         load(wd_in.at[:, pl.ds(i * wd_rows, wd_rows)], wd.at[:, pl.ds(i * wd_rows, wd_rows)])
@@ -109,10 +109,10 @@
             return send(view(y, z, p, h), view(y, z, p, h), device)
 
         first = view(y0, z0, None, None) if own is None else own
-        near = [
-            send(first, view(y0, z0, None, None), device)
-            for device in (Y_UP, Z_UP, Y_DOWN, Z_DOWN, Y_OPP, Z_OPP)
-        ]
+        target = view(y0, z0, None, None)
+        near = [send(first, target, device) for device in (Y_UP, Z_UP, Y_DOWN, Z_DOWN)]
+        yield
+        near += [send(first, target, device) for device in (Y_OPP, Z_OPP)]
         yield
         a, b = [], []
         for k, i, j in ((0, ym, zm), (2, yp, zp)):
@@ -136,7 +136,8 @@
             last.append(hand(y, zp, 0, 1, Z_DOWN))
             b[2 * i + 1].wait_recv()
             last.append(hand(yp, z, 1, 1, Y_DOWN))
-        yield
+            if i:
+                yield
         for copy in last:
             copy.wait_recv()
         yield
@@ -240,6 +241,7 @@
     gather_own = gather_small(0, neighbours=True)
     gather_opp = gather_small(1)
     passed = next(gather_own)
+    next(gather_x)
     for copy in load_rest:
         copy.wait()
     for copy in weight_copies:
@@ -247,15 +249,16 @@
     for h in range(2):
         wqh[h], wql[h] = split(wq[h])
     next(gather_x)
+    next(gather_own)
     next(gather_x)
-    next(gather_own)
+    across.wait_recv()
+    next(gather_opp)
     next(gather_x)
     for h in range(2):
         wuh[h], wul[h] = split(wu[h])
-    across.wait_recv()
-    next(gather_opp)
     next(gather_own)
     made = {0: make(0, [(0, None)])}
+    next(gather_x)
     next(gather_opp)
     woh[...], wol[...] = split(wo[...].reshape(2 * VDIM, D))
     next(gather_x)
@@ -325,25 +328,29 @@
     )
     near = ["own", ("y", 0), ("y", 1), ("y", 2), ("z", 0), (0, 0), (1, 0), (2, 0)]
     far = [(name, j) for j in (1, 2) for name in ("z", 0, 1, 2)]
-    attend(kv[0], positions(chunks[0]) + core * 16)
+    def near_side(g):
+        attend(kv[g], positions(chunks[g]) + core * 16)
+
+    def far_side(g):
+        made[g].wait_recv()
+        attend(kv_far[g], positions(chunks[g]) + (1 - core) * 16)
+
+    near_side(0)
+    arrive(near)
+    made[2] = make(2, chunks[2])
+    far_side(0)
+    near_side(2)
     next(gather_opp)
     made[1] = make(1, chunks[1])
-    made[0].wait_recv()
-    attend(kv_far[0], positions(chunks[0]) + (1 - core) * 16)
-    attend(kv[1], positions(chunks[1]) + core * 16)
-    arrive(near)
-    made[2] = make(2, chunks[2])
-    made[1].wait_recv()
-    attend(kv_far[1], positions(chunks[1]) + (1 - core) * 16)
-    attend(kv[2], positions(chunks[2]) + core * 16)
+    far_side(2)
+    near_side(1)
     arrive(far)
     made[3] = make(3, chunks[3])
-    made[2].wait_recv()
-    attend(kv_far[2], positions(chunks[2]) + (1 - core) * 16)
-    attend(kv[3], positions(chunks[3]) + core * 16)
-    made[3].wait_recv()
-    attend(kv_far[3], positions(chunks[3]) + (1 - core) * 16)
-
+    far_side(1)
+    near_side(3)
+    far_side(3)
+
+    gathered = len(copies)
     heads = []
     for h in range(2):
         ln[h] = jnp.broadcast_to(top[h] + jnp.log(tot[h]), (8, 256))
@@ -407,6 +414,8 @@
             device = (opposite, down, upward)[i]
             final2[p, i] = send(red.at[p, i], sums2.at[p, i], device)
 
+    for copy in copies[:gathered]:
+        copy.wait_send()
     for i in range(4):
         for p in range(2):
             pass_on(p, i)
@@ -440,7 +449,7 @@
         stores.append(load(rows_out.at[:, :, cols], out.at[:, :, cols]))
     for copy in stores:
         copy.wait()
-    for copy in copies:
+    for copy in copies[gathered:]:
         copy.wait_send()
 
 

time: 65.9 us -> 64.8 us (0.983); the launches traced: 65.7 us -> 63.7 us
  Pallas kernels: 62.3 us -> 60.2 us
    pallas_call x1, Pallas kernels: 62.3 us -> 60.2 us  [body(): pl.pallas_call(kernel, out_shape=(jax.ShapeDtypeStruct((2, 8, D), f32), j...]
where the time goes in v6:
time: 64.8 us; the launch traced here: 63.7 us
  Pallas kernels  60.2 us (93%)
  local copies, waits for them, and re-layouts  2.81 us (4%)
    pallas_call x1, Pallas kernels, body(): pl.pallas_call(kernel, out_shape=(jax.ShapeDtypeStruct((2, 8, D), f32), j...  60.2 us
    unnamed x2, local copies, waits for them, and re-layouts  2.81 us

profile of v6, /device:TPU:0, one launch (start us, length us, event | category | flops | bytes accessed | tf_op | source)
XLA Modules:
  0.0 63.7 jit_solution(9149067200074890937)
XLA Ops:
  0.6 60.2 %latent_attention.1 = (f32[2,8,2304]{2,1,0:T(8,128)}, f32[1,512]{1,0:T(1,128)}) custom-call(f32[2,8,2304]{2,1,0:T(8,128)} %bitcast.8, s32[16,128]{1,0:T(8,128)} %bitcast.9, f32[192,2304]{1,0:T(8,128)} %bitcast.6, f32[576,2304]{1,0:T(8,128)} %bitcast.5, f32[512,256]{1,0:T(8,128)} %wu_in.1, f32[128,2304]{1,0:T(8,128)} %wo_in.1), custom_call_target="tpu_custom_call" | custom-call | tf_op jit(solution)/shard_map/latent_attention/pallas_call | solution.py:458
  60.8 1.6 %copy.10 = f32[16,2304]{1,0:T(8,128)} copy(f32[16,2304]{1,0:T(8,128)} %bitcast.7) | data formatting | bytes 294912
  62.4 1.2 %copy.11 = f32[1,512]{1,0:T(1,128)} copy(f32[1,512]{1,0:T(1,128)} %get-tuple-element.9) | data formatting | bytes 4096

commit v7 on v6

--- a/solution.py
+++ b/solution.py
@@ -329,26 +329,26 @@
     near = ["own", ("y", 0), ("y", 1), ("y", 2), ("z", 0), (0, 0), (1, 0), (2, 0)]
     far = [(name, j) for j in (1, 2) for name in ("z", 0, 1, 2)]
     def near_side(g):
-        attend(kv[g], positions(chunks[g]) + core * 16)
+        return kv[g], positions(chunks[g]) + core * 16
 
     def far_side(g):
         made[g].wait_recv()
-        attend(kv_far[g], positions(chunks[g]) + (1 - core) * 16)
-
-    near_side(0)
+        return kv_far[g], positions(chunks[g]) + (1 - core) * 16
+
+    def attend_both(one, two):
+        attend(*(jnp.concatenate(pair, axis=0) for pair in zip(one, two)))
+
+    attend(*near_side(0))
     arrive(near)
     made[2] = make(2, chunks[2])
-    far_side(0)
-    near_side(2)
+    attend_both(far_side(0), near_side(2))
     next(gather_opp)
     made[1] = make(1, chunks[1])
-    far_side(2)
-    near_side(1)
+    attend_both(far_side(2), near_side(1))
     arrive(far)
     made[3] = make(3, chunks[3])
-    far_side(1)
-    near_side(3)
-    far_side(3)
+    attend_both(far_side(1), near_side(3))
+    attend(*far_side(3))
 
     gathered = len(copies)
     heads = []

time: 64.8 us -> 64.1 us (0.989)
  no operation moved by 1% of the time
where the time goes in v7:
time: 64.1 us; the launch traced here: 63.3 us
  Pallas kernels  59.9 us (93%)
  local copies, waits for them, and re-layouts  2.81 us (4%)
    pallas_call x1, Pallas kernels, body(): pl.pallas_call(kernel, out_shape=(jax.ShapeDtypeStruct((2, 8, D), f32), j...  59.9 us
    unnamed x2, local copies, waits for them, and re-layouts  2.81 us

profile of v7, /device:TPU:0, one launch (start us, length us, event | category | flops | bytes accessed | tf_op | source)
XLA Modules:
  0.0 63.3 jit_solution(7084717862050622422)
XLA Ops:
  0.6 59.9 %latent_attention.1 = (f32[2,8,2304]{2,1,0:T(8,128)}, f32[1,512]{1,0:T(1,128)}) custom-call(f32[2,8,2304]{2,1,0:T(8,128)} %bitcast.8, s32[16,128]{1,0:T(8,128)} %bitcast.9, f32[192,2304]{1,0:T(8,128)} %bitcast.6, f32[576,2304]{1,0:T(8,128)} %bitcast.5, f32[512,256]{1,0:T(8,128)} %wu_in.1, f32[128,2304]{1,0:T(8,128)} %wo_in.1), custom_call_target="tpu_custom_call" | custom-call | tf_op jit(solution)/shard_map/latent_attention/pallas_call | solution.py:458
  60.5 1.6 %copy.10 = f32[16,2304]{1,0:T(8,128)} copy(f32[16,2304]{1,0:T(8,128)} %bitcast.7) | data formatting | bytes 294912
  62.1 1.2 %copy.11 = f32[1,512]{1,0:T(1,128)} copy(f32[1,512]{1,0:T(1,128)} %get-tuple-element.9) | data formatting | bytes 4096

commit v8 on v7

--- a/solution.py
+++ b/solution.py
@@ -382,8 +382,8 @@
 
     for p in range(2):
         (um, u0, up, uo), down, upward, _ = axes[p]
-        tile = HALF // 3
-        for t in range(3):
+        tile = HALF
+        for t in range(1):
             cols = pl.ds(p * HALF + t * tile, tile)
             part[:, :, :, :, cols] = dot3(rows, (woh[:, cols], wol[:, cols])).reshape(4, 4, 2, 8, tile)
         for i in range(4):

time: 64.1 us -> 63.9 us (level)
  no operation moved by 1% of the time
where the time goes in v8:
time: 63.9 us; the launch traced here: 63.2 us
  Pallas kernels  59.8 us (94%)
  local copies, waits for them, and re-layouts  2.81 us (4%)
  between operations  0.64 us (1%)
    pallas_call x1, Pallas kernels, body(): pl.pallas_call(kernel, out_shape=(jax.ShapeDtypeStruct((2, 8, D), f32), j...  59.8 us
    unnamed x2, local copies, waits for them, and re-layouts  2.81 us

profile of v8, /device:TPU:0, one launch (start us, length us, event | category | flops | bytes accessed | tf_op | source)
XLA Modules:
  0.0 63.2 jit_solution(9193188644972011110)
XLA Ops:
  0.6 59.8 %latent_attention.1 = (f32[2,8,2304]{2,1,0:T(8,128)}, f32[1,512]{1,0:T(1,128)}) custom-call(f32[2,8,2304]{2,1,0:T(8,128)} %bitcast.8, s32[16,128]{1,0:T(8,128)} %bitcast.9, f32[192,2304]{1,0:T(8,128)} %bitcast.6, f32[576,2304]{1,0:T(8,128)} %bitcast.5, f32[512,256]{1,0:T(8,128)} %wu_in.1, f32[128,2304]{1,0:T(8,128)} %wo_in.1), custom_call_target="tpu_custom_call" | custom-call | tf_op jit(solution)/shard_map/latent_attention/pallas_call | solution.py:458
  60.4 1.6 %copy.10 = f32[16,2304]{1,0:T(8,128)} copy(f32[16,2304]{1,0:T(8,128)} %bitcast.7) | data formatting | bytes 294912
  62.0 1.2 %copy.11 = f32[1,512]{1,0:T(1,128)} copy(f32[1,512]{1,0:T(1,128)} %get-tuple-element.9) | data formatting | bytes 4096
